TPU v7x, 128 devices: a whole 4x4x4 slice. The times are simulated.
128 devices in a mesh: dp: 32 (over z, y, core), head: 4 (over x).
Axes of the slice: x: 4, y: 4, z: 4, core: 2. Of those that a mesh axis runs over, the one named last changes fastest.
Arguments:
- hidden: bfloat16 [16384, 4096], P('dp', 'head'), may hold values from -10 to 10
- query_weight: bfloat16 [4096, 2048], P('head'), as said below
- key_weight: bfloat16 [4096, 2048], P(None, 'head'), as said below
- value_weight: bfloat16 [4096, 2048], P(None, 'head'), may hold values from -0.09375 to 0.09375
- output_weight: bfloat16 [2048, 4096], P(None, 'head'), may hold values from -0.125 to 0.125
- encoded: bfloat16 [128, 128, 4096], P('dp'), may hold values from -10 to 10
- location: int32 [128], replicated, may hold values from 0 to 127, as said below
- neighbours: int32 [256, 2], P('dp'), may hold values from 0 to 127, as said below
- pattern: int32 [256, 2], P('dp'), may hold values from 0 to 1, as said below
- grad_out: bfloat16 [16384, 4096], P('dp', 'head'), may hold values from -6 to 6
Outputs:
- attended: bfloat16 [16384, 4096], P('dp', 'head')
- grad_hidden: bfloat16 [16384, 4096], P('dp', 'head')
- grad_encoded: bfloat16 [128, 128, 4096], P(('dp', 'head'))
Inputs may be any that keep to these rules, and one draw needn't show every extreme that they name: A permutation: the encoded tokens of database row r are encoded[location[r]]. `neighbours`: database row ids. Group the storage indices into aligned blocks of 4 (same s // 4); for every sequence, at most 2 of its 16 entries name rows stored in one block, and they name at most 1 distinct rows; in every draw each sequence names some row twice. `pattern`: every span attends at least one neighbour. `query_weight`: entries of order 4096 ** -0.5. `key_weight`: entries of order 4096 ** -0.5.
All inputs are finite; a program needn't handle non-finite values.
Results may differ from a plain program's by a relative error of at most 0.04.
Values may be sent and summed in bfloat16 or wider, within the bound.
A program may use at most 192 MiB of HBM per device.

v0:
```python
import jax
import jax.numpy as jnp
from jax import lax
from jax.sharding import PartitionSpec as P

HD = 128
SPAN = 64
NTOK = 128
NBR = 2
ROW_CAP = 1


def shift_up(tensor_in):
    padding = jnp.zeros((SPAN - 1,) + tensor_in.shape[1:], tensor_in.dtype)
    return jnp.concatenate([tensor_in[SPAN - 1 :], padding], axis=0)


def shift_down(tensor_in):
    padding = jnp.zeros((SPAN - 1,) + tensor_in.shape[1:], tensor_in.dtype)
    return jnp.concatenate([padding, tensor_in[: tensor_in.shape[0] - SPAN + 1]], axis=0)


def slot_plan(row_ids, location, rows_dev):
    stored = jnp.take(location, row_ids, axis=0)
    source = stored // rows_dev
    local = stored % rows_dev
    slot_count = row_ids.shape[-1]
    before = jnp.arange(slot_count)[None, :] < jnp.arange(slot_count)[:, None]
    same_source = source[..., :, None] == source[..., None, :]
    same_row = stored[..., :, None] == stored[..., None, :]
    slot_rank = jnp.sum(before & same_source, axis=-1)
    is_first = jnp.logical_not(jnp.any(before & same_row, axis=-1))
    first_index = jnp.argmax(same_row, axis=-1)
    earlier_first = jnp.arange(slot_count)[None, :] < first_index[..., :, None]
    row_rank = jnp.sum(earlier_first & same_source & is_first[..., None, :], axis=-1)
    return (source, local, slot_rank, row_rank)


def source_table(source, local, rank, target, capacity):
    matches = (source[..., None] == target) & (rank[..., None] == jnp.arange(capacity))
    return jnp.max(jnp.where(matches, local[..., None], -1), axis=-2)


def body(
    hidden,
    query_weight,
    key_weight,
    value_weight,
    output_weight,
    encoded,
    location,
    neighbours,
    pattern,
    grad_out,
):
    n_dp = lax.axis_size("dp")
    own_index = lax.axis_index("dp")
    seq_len = hidden.shape[0]
    spans_dev = neighbours.shape[0]
    rows_dev = encoded.shape[0]
    group_width = key_weight.shape[1]
    heads_dev = group_width // HD
    slot_count = spans_dev * NBR
    score_scale = HD ** (-0.5)
    partial_queries = jnp.dot(hidden, query_weight, preferred_element_type=jnp.float32)
    queries = lax.psum_scatter(
        partial_queries.astype(jnp.bfloat16), "head", scatter_dimension=1, tiled=True
    )
    state_rows = encoded.reshape(rows_dev * NTOK, encoded.shape[2])
    key_rows = jnp.dot(state_rows, key_weight, preferred_element_type=jnp.float32).astype(
        jnp.bfloat16
    )
    value_rows = jnp.dot(state_rows, value_weight, preferred_element_type=jnp.float32).astype(
        jnp.bfloat16
    )
    paired_rows = jnp.concatenate([key_rows, value_rows], axis=1).reshape(
        rows_dev, NTOK, 2 * group_width
    )
    own_source, own_local, own_slot_rank, own_row_rank = slot_plan(
        neighbours.reshape(1, -1), location, rows_dev
    )
    every_ids = lax.all_gather(neighbours, "dp", axis=0, tiled=True).reshape(n_dp, -1)
    source, local, slot_rank, row_rank = slot_plan(every_ids, location, rows_dev)
    row_table = source_table(source, local, row_rank, own_index, ROW_CAP)
    outgoing = jnp.take(paired_rows, jnp.maximum(row_table, 0), axis=0)
    arrived = lax.all_to_all(outgoing, "dp", split_axis=0, concat_axis=0, tiled=True)
    flat_index = own_source[0] * ROW_CAP + own_row_rank[0]
    memory = jnp.take(arrived.reshape(-1, NTOK, 2 * group_width), flat_index, axis=0)
    memory = memory.reshape(spans_dev, NBR * NTOK, 2, heads_dev, HD)
    key_memory = memory[:, :, 0]
    value_memory = memory[:, :, 1]
    query_block = shift_up(queries).reshape(spans_dev, SPAN, heads_dev, HD)
    scores = (
        jnp.einsum("cqhd,cmhd->chqm", query_block, key_memory, preferred_element_type=jnp.float32)
        * score_scale
    )
    live_mask = jnp.repeat(pattern, NTOK, axis=1)[:, None, None, :] > 0
    masked = jnp.where(live_mask, scores, -1e30)
    row_max = jnp.max(masked, axis=-1, keepdims=True)
    exp_terms = jnp.where(live_mask, jnp.exp(masked - row_max), 0.0)
    soft_weights = exp_terms / jnp.sum(exp_terms, axis=-1, keepdims=True)
    rounded = soft_weights.astype(jnp.bfloat16)
    blended = jnp.einsum(
        "chqm,cmhd->cqhd", rounded, value_memory, preferred_element_type=jnp.float32
    ).astype(jnp.bfloat16)
    blended = shift_down(blended.reshape(seq_len, group_width))
    attended = jnp.dot(
        lax.all_gather(blended, "head", axis=1, tiled=True),
        output_weight,
        preferred_element_type=jnp.float32,
    ).astype(jnp.bfloat16)
    partial_grad = lax.dot_general(
        grad_out, output_weight, (((1,), (1,)), ((), ())), preferred_element_type=jnp.float32
    )
    grad_blended = lax.psum_scatter(
        partial_grad.astype(jnp.bfloat16), "head", scatter_dimension=1, tiled=True
    )
    grad_block = shift_up(grad_blended).reshape(spans_dev, SPAN, heads_dev, HD)
    grad_weights = jnp.einsum(
        "cqhd,cmhd->chqm", grad_block, value_memory, preferred_element_type=jnp.float32
    )
    inner_sum = jnp.sum(soft_weights * grad_weights, axis=-1, keepdims=True)
    grad_scores = (soft_weights * (grad_weights - inner_sum) * score_scale).astype(jnp.bfloat16)
    grad_queries = jnp.einsum(
        "chqm,cmhd->cqhd", grad_scores, key_memory, preferred_element_type=jnp.float32
    ).astype(jnp.bfloat16)
    grad_queries = shift_down(grad_queries.reshape(seq_len, group_width))
    key_slot = jnp.einsum(
        "chqm,cqhd->cmhd", grad_scores, query_block, preferred_element_type=jnp.float32
    )
    value_slot = jnp.einsum(
        "chqm,cqhd->cmhd", rounded, grad_block, preferred_element_type=jnp.float32
    )
    slot_grads = jnp.concatenate(
        [
            key_slot.reshape(slot_count, NTOK, group_width),
            value_slot.reshape(slot_count, NTOK, group_width),
        ],
        axis=2,
    ).reshape(slot_count, -1)
    entry_index = own_source[0] * ROW_CAP + own_row_rank[0]
    assign = (jnp.arange(n_dp * ROW_CAP)[:, None] == entry_index[None, :]).astype(jnp.float32)
    per_row = jnp.dot(
        assign, slot_grads, precision=lax.Precision.HIGHEST, preferred_element_type=jnp.float32
    )
    sending = per_row.astype(jnp.bfloat16).reshape(n_dp, ROW_CAP, NTOK, 2 * group_width)
    returned = lax.all_to_all(sending, "dp", split_axis=0, concat_axis=0, tiled=True)
    collect = (jnp.arange(rows_dev)[:, None] == row_table.reshape(1, -1)).astype(jnp.bfloat16)
    row_sum = jnp.dot(
        collect, returned.reshape(n_dp * ROW_CAP, -1), preferred_element_type=jnp.float32
    )
    row_sum = row_sum.astype(jnp.bfloat16).reshape(rows_dev, NTOK, 2 * group_width)
    key_grad = row_sum[:, :, :group_width]
    value_grad = row_sum[:, :, group_width:]
    term_keys = jnp.einsum("rtk,dk->rtd", key_grad, key_weight, preferred_element_type=jnp.float32)
    grad_encoded = lax.psum_scatter(
        (
            term_keys
            + jnp.einsum(
                "rtk,dk->rtd", value_grad, value_weight, preferred_element_type=jnp.float32
            )
        ).astype(jnp.bfloat16),
        "head",
        scatter_dimension=0,
        tiled=True,
    )
    grad_hidden = lax.dot_general(
        lax.all_gather(grad_queries, "head", axis=1, tiled=True),
        query_weight,
        (((1,), (1,)), ((), ())),
        preferred_element_type=jnp.float32,
    ).astype(jnp.bfloat16)
    return (attended, grad_hidden, grad_encoded)


def solution(mesh):
    return jax.shard_map(
        body,
        mesh=mesh,
        in_specs=(
            P("dp", "head"),
            P("head", None),
            P(None, "head"),
            P(None, "head"),
            P(None, "head"),
            P("dp", None, None),
            P(),
            P("dp", None),
            P("dp", None),
            P("dp", "head"),
        ),
        out_specs=(P("dp", "head"), P("dp", "head"), P(("dp", "head"), None, None)),
        check_vma=False,
    )
```

profile of v0, /device:TPU:1, one launch (start us, length us, event | category | flops | bytes accessed | tf_op | source)
XLA Modules:
  0.0 471.6 jit_solution(8455605207952738214)
XLA Ops:
  7.2 1.2 copy-done
  8.4 5.9 %convolution_convert_fusion.3 = bf16[512,2048]{1,0:T(8,128)(2,1)} fusion(bf16[512,1024]{1,0:T(8,128)(2,1)S(1)} %copy-done, bf16[1024,2048]{1,0:T(8,128)(2,1)} %param.11), kind=kOutput, calls=%fused_computation.17 | convolution fusion | flops 2148532224 | bytes 7340032 | tf_op jit(solution)/shard_map/dot_general | solution.py:65
  14.3 27.0 %all-gather = s32[32,8,2]{1,2,0:T(2,128)S(1)} all-gather(s32[1,8,2]{1,2,0:T(2,128)S(1)} %bitcast.130), channel_id=1, replica_groups=mesh['dp'=32,'head'=4] {'dp'}, dimensions={0}, use_global_device_ids=true | all-gather | bytes 2112 | tf_op jit(solution)/shard_map/all_gather | solution.py:82
  41.6 3.3 gather_fusion.1
  45.3 0.7 compare_reduce_fusion
  46.9 6.0 %convolution_convert_fusion.6 = bf16[512,512]{0,1:T(8,128)(2,1)S(1)} fusion(bf16[512,4096]{1,0:T(8,128)(2,1)} %bitcast.132, bf16[4096,512]{1,0:T(8,128)(2,1)} %param.13), kind=kOutput, calls=%fused_computation.36 | convolution fusion | flops 2147745792 | bytes 8912896 | tf_op jit(solution)/shard_map/dot_general | solution.py:73
  53.0 2.4 convolution_convert_fusion.7
  55.4 0.5 copy.157
  56.0 4.8 %gather_fusion.2 = bf16[32,128,1024]{2,1,0:T(8,128)(2,1)} fusion(bf16[4,128,1024]{2,1,0:T(8,128)(2,1)S(1)} %bitcast.116, s32[1024]{0:T(1024)S(1)} %pad_clamp_fusion.1), kind=kCustom, calls=%fused_computation.2 | custom fusion | bytes 16777344 | tf_op jit(solution)/shard_map/jit(_take)/gather | solution.py:85
  60.8 7.5 %fusion.2 = bf16[32,1,128,1024]{3,2,1,0:T(8,128)(2,1)} fusion(bf16[32,128,1024]{2,1,0:T(8,128)(2,1)} %gather_fusion.2, pred[32]{0:T(512)(128)(4,1)S(1)} %broadcast_compare_fusion.2), kind=kLoop, calls=%fused_computation.10 | loop fusion | flops 4194304 | bytes 16777248 | tf_op jit(solution)/shard_map/jit(_take)/select_n | solution.py:85
  68.3 5.2 %all-to-all-start = ((bf16[32,1,128,1024]{3,2,1,0:T(8,128)(2,1)}), bf16[32,1,128,1024]{3,2,1,0:T(8,128)(2,1)}, u32[]{:S(2)}, u32[]{:S(2)}) async-start(bf16[32,1,128,1024]{3,2,1,0:T(8,128)(2,1)} %fusion.2), calls=%async_computation | async-start | bytes 16777216 | tf_op jit(solution)/shard_map/all_to_all | solution.py:86
  73.7 5.9 %convolution_convert_fusion.2 = bf16[512,2048]{1,0:T(8,128)(2,1)} fusion(bf16[512,1024]{1,0:T(8,128)(2,1)S(1)} %copy-done.11, bf16[2048,1024]{1,0:T(8,128)(2,1)} %param.14), kind=kOutput, calls=%fused_computation.16 | convolution fusion | flops 2148532224 | bytes 7340032 | tf_op jit(solution)/shard_map/dot_general | solution.py:112
  80.0 0.7 gather_fusion
  80.9 0.7 compare_reduce_fusion.1
  82.4 1.1 slice.40
  83.6 0.9 reshape.884
  84.5 25.9 %reduce-scatter.6.cloned.1.call-done = bf16[512,512]{1,0:T(8,128)(2,1)} async-done(((bf16[512,2048]{1,0:T(8,128)(2,1)}), bf16[512,512]{1,0:T(8,128)(2,1)}) %reduce-scatter.6.cloned.1.call-update) | async-done | bytes 524304 | tf_op jit(solution)/shard_map/reduce_scatter | solution.py:115
  110.4 1.1 slice.44
  111.7 61.5 %all-to-all-done = bf16[32,1,128,1024]{3,2,1,0:T(8,128)(2,1)} async-done(((bf16[32,1,128,1024]{3,2,1,0:T(8,128)(2,1)}), bf16[32,1,128,1024]{3,2,1,0:T(8,128)(2,1)}, u32[]{:S(2)}, u32[]{:S(2)}) %all-to-all-start) | async-done | bytes 8388640 | tf_op jit(solution)/shard_map/all_to_all | solution.py:86
  173.2 6.2 %gather_fusion.3 = bf16[16,128,1024]{2,1,0:T(8,128)(2,1)} fusion(bf16[32,128,1024]{2,1,0:T(8,128)(2,1)} %bitcast.10, s32[1024]{0:T(1024)S(1)} %pad_clamp_fusion), kind=kCustom, calls=%fused_computation.3 | custom fusion | bytes 8388672 | tf_op jit(solution)/shard_map/jit(_take)/gather | solution.py:88
  179.4 7.7 %reshape.938 = bf16[8,256,2,4,128]{4,3,2,1,0:T(4,128)(2,1)} reshape(bf16[16,128,1024]{2,1,0:T(8,128)(2,1)} %gather_fusion.3) | data formatting | bytes 8388608 | tf_op jit(solution)/shard_map/jit(_take)/gather | solution.py:88
  187.1 2.9 copy_select_fusion
  190.0 1.9 copy-done.3
  191.9 0.9 fusion.12
  193.0 3.9 fusion.61
  196.9 4.4 convolution_bitcast_fusion
  201.3 15.9 %convolution_bitcast_fusion.1 = f32[8,256,4,128]{1,3,2,0:T(8,128)} fusion(f32[8,4,64,256]{3,2,1,0:T(8,128)S(1)} %fusion.12, bf16[8,64,4,128]{3,2,1,0:T(4,128)(2,1)S(1)} %copy-done.7, f32[8,4,64,256]{3,2,1,0:T(8,128)} %get-tuple-element.12, f32[8,4,64]{2,1,0:T(4,128)S(1)} %get-tuple-element.11), kind=kOutput, calls=%fused_computation.19 | convolution fusion | flops 137890048 | bytes 8921088 | tf_op jit(solution)/shard_map/chqm,cqhd->cmhd/dot_general | solution.py:128
  217.2 6.6 %copy.152 = f32[8,256,4,128]{1,0,3,2:T(8,128)} copy(f32[8,256,4,128]{1,3,2,0:T(8,128)} %convolution_bitcast_fusion.1) | data formatting | bytes 8388608 | tf_op jit(solution)/shard_map/chqm,cqhd->cmhd/transpose | solution.py:128
  223.8 4.9 %reshape.888 = f32[16,128,512]{1,0,2:T(8,128)} reshape(f32[8,256,4,128]{1,0,3,2:T(8,128)} %copy.152) | data formatting | bytes 8388608 | tf_op jit(solution)/shard_map/reshape | solution.py:136
  228.7 6.6 %copy.154 = f32[8,256,4,128]{1,0,3,2:T(8,128)} copy(f32[8,256,4,128]{1,3,2,0:T(8,128)} %convolution_bitcast_fusion) | data formatting | bytes 8388608 | tf_op jit(solution)/shard_map/chqm,cqhd->cmhd/transpose | solution.py:131
  235.3 4.7 %reshape.889 = f32[16,128,512]{1,0,2:T(8,128)} reshape(f32[8,256,4,128]{1,0,3,2:T(8,128)} %copy.154) | data formatting | bytes 8388608 | tf_op jit(solution)/shard_map/reshape | solution.py:137
  240.0 7.2 %fusion.62 = f32[2,8,128,1024]{2,1,0,3:T(8,128)} fusion(f32[16,128,512]{1,0,2:T(8,128)} %reshape.889, f32[16,128,512]{1,0,2:T(8,128)} %reshape.888), kind=kLoop, calls=%fused_computation.142 | loop fusion | flops 2097152 | bytes 16777216
  247.2 8.8 %copy.162 = f32[2,8,128,1024]{3,1,2,0:T(8,128)} copy(f32[2,8,128,1024]{2,1,0,3:T(8,128)} %fusion.62) | data formatting | bytes 16777216
  256.0 14.1 %convolution_convert_fusion = bf16[32,131072]{1,0:T(8,128)(2,1)} fusion(f32[16,131072]{1,0:T(8,128)} %bitcast.118, s32[16]{0:T(128)S(1)} %add.228), kind=kOutput, calls=%fused_computation.6 | convolution fusion | flops 809501184 | bytes 16777280 | tf_op jit(solution)/shard_map/dot_general | solution.py:143
  270.1 11.3 %copy.163 = bf16[4,8,128,1024]{3,2,1,0:T(8,128)(2,1)} copy(bf16[4,8,128,1024]{3,1,2,0:T(8,128)(2,1)} %bitcast.119) | data formatting | bytes 16777216
  281.5 11.0 %all-to-all-start.1 = ((bf16[32,1,128,1024]{3,2,1,0:T(8,128)(2,1)}), bf16[32,1,128,1024]{3,2,1,0:T(8,128)(2,1)}, u32[]{:S(2)}, u32[]{:S(2)}) async-start(bf16[32,1,128,1024]{3,2,1,0:T(8,128)(2,1)} %bitcast.120), calls=%async_computation.3 | async-start | bytes 16777216 | tf_op jit(solution)/shard_map/all_to_all | solution.py:147
  292.5 14.1 %fusion.23 = bf16[8,64,4,128]{3,1,2,0:T(8,128)(2,1)S(1)} fusion(bf16[8,256,2,4,128]{4,1,3,0,2:T(8,128)(2,1)} %copy-done.3, f32[8,4,64,256]{3,2,1,0:T(8,128)S(1)} %fusion.12, f32[8,4,64,256]{3,2,1,0:T(8,128)} %get-tuple-element.12, f32[8,4,64]{2,1,0:T(4,128)S(1)} %get-tuple-element.11), kind=kOutput, calls=%fused_computation.39 | convolution fusion | flops 138152192 | bytes 11042816 | tf_op jit(solution)/shard_map/chqm,cmhd->cqhd/dot_general | solution.py:124
  307.2 0.9 concatenate.22
  308.2 2.1 fusion.22
  310.9 0.9 concatenate.20
  312.0 80.2 %all-to-all-done.1 = bf16[32,1,128,1024]{3,2,1,0:T(8,128)(2,1)} async-done(((bf16[32,1,128,1024]{3,2,1,0:T(8,128)(2,1)}), bf16[32,1,128,1024]{3,2,1,0:T(8,128)(2,1)}, u32[]{:S(2)}, u32[]{:S(2)}) %all-to-all-start.1) | async-done | bytes 8388640 | tf_op jit(solution)/shard_map/all_to_all | solution.py:147
  392.3 11.4 %copy.164 = bf16[4,8,128,1024]{3,1,2,0:T(8,128)(2,1)} copy(bf16[4,8,128,1024]{3,2,1,0:T(8,128)(2,1)} %bitcast.43) | data formatting | bytes 16777216
  403.7 4.7 %convolution_convert_fusion.1 = bf16[4,131072]{1,0:T(4,128)(2,1)S(1)} fusion(bf16[32,131072]{1,0:T(8,128)(2,1)} %bitcast.117, s32[32]{0:T(128)S(1)} %reduce_max.27), kind=kOutput, calls=%fused_computation.7 | convolution fusion | flops 34078848 | bytes 9437312 | tf_op jit(solution)/shard_map/dot_general | solution.py:149
  408.7 2.4 fusion.4
  411.1 4.3 add_convert_fusion
  415.5 6.2 %convolution_convert_fusion.4 = bf16[512,1024]{1,0:T(8,128)(2,1)} fusion(bf16[512,2048]{1,0:T(8,128)(2,1)} %all-gather.6.cloned.1.call-done, bf16[1024,2048]{1,0:T(8,128)(2,1)} %param.11), kind=kOutput, calls=%fused_computation.32 | convolution fusion | flops 2148007936 | bytes 7340032 | tf_op jit(solution)/shard_map/dot_general | solution.py:167
  421.7 6.2 %convolution_convert_fusion.5 = bf16[512,1024]{1,0:T(8,128)(2,1)} fusion(bf16[512,2048]{1,0:T(8,128)(2,1)} %all-gather.4.cloned.1.call-done, bf16[2048,1024]{1,0:T(8,128)(2,1)} %param.14), kind=kOutput, calls=%fused_computation.33 | convolution fusion | flops 2148007936 | bytes 7340032 | tf_op jit(solution)/shard_map/dot_general | solution.py:107
  427.9 37.0 %reduce-scatter.8.cloned.1.call-done = bf16[1,128,4096]{2,1,0:T(8,128)(2,1)} async-done(((bf16[4,128,4096]{2,1,0:T(8,128)(2,1)}), bf16[1,128,4096]{2,1,0:T(8,128)(2,1)}) %reduce-scatter.8.cloned.1.call-update) | async-done | bytes 1048592 | tf_op jit(solution)/shard_map/reduce_scatter | solution.py:156
  (96 shorter events, 5.4 us)
Async XLA Ops:
  7.2 1.2 copy-start
  7.2 7.1 %copy-start.8 = (s32[8,2]{0,1:T(2,128)S(1)}, s32[8,2]{0,1:T(2,128)}, u32[]{:S(2)}) copy-start(s32[8,2]{0,1:T(2,128)} %param.17) | copy-start | bytes 196
  7.2 75.2 %reduce-scatter.4.cloned.1.call-start = ((), (), s32[]{:S(2)}) async-start(), calls=%async_computation.5 | async-start | bytes 2621440 | tf_op jit(solution)/shard_map/reduce_scatter | solution.py:66
  14.3 27.3 %copy-start.2 = (s32[128]{0:T(128)S(1)}, s32[128]{0:T(128)}, u32[]{:S(2)}) copy-start(s32[128]{0:T(128)} %param.16) | copy-start | bytes 1540
  46.9 6.0 %copy-start.4 = (bf16[4096,512]{1,0:T(8,128)(2,1)S(1)}, bf16[4096,512]{1,0:T(8,128)(2,1)}, u32[]{:S(2)}) copy-start(bf16[4096,512]{1,0:T(8,128)(2,1)} %param.12) | copy-start | bytes 12582916
  46.9 6.0 %copy-start.10 = (bf16[4,128,4096]{2,1,0:T(8,128)(2,1)S(1)}, bf16[4,128,4096]{2,1,0:T(8,128)(2,1)}, u32[]{:S(2)}) copy-start(bf16[4,128,4096]{2,1,0:T(8,128)(2,1)} %param.15) | copy-start | bytes 12582916
  68.3 5.5 %copy-start.11 = (bf16[512,1024]{1,0:T(8,128)(2,1)S(1)}, bf16[512,1024]{1,0:T(8,128)(2,1)}, u32[]{:S(2)}) copy-start(bf16[512,1024]{1,0:T(8,128)(2,1)} %param.19) | copy-start | bytes 3145732
  68.3 105.0 %all-to-all-start = ((bf16[32,1,128,1024]{3,2,1,0:T(8,128)(2,1)}), bf16[32,1,128,1024]{3,2,1,0:T(8,128)(2,1)}, u32[]{:S(2)}, u32[]{:S(2)}) async-start(bf16[32,1,128,1024]{3,2,1,0:T(8,128)(2,1)} %fusion.2), calls=%async_computation | async-start | bytes 16777216 | tf_op jit(solution)/shard_map/all_to_all | solution.py:86
  73.5 8.5 %copy-start.9 = (s32[8,2]{0,1:T(2,128)S(1)}, s32[8,2]{0,1:T(2,128)}, u32[]{:S(2)}) copy-start(s32[8,2]{0,1:T(2,128)} %param.18) | copy-start | bytes 196
  73.5 36.9 %reduce-scatter.6.cloned.1.call-start = ((), (), s32[]{:S(2)}) async-start(), calls=%async_computation.7 | async-start | bytes 2621440 | tf_op jit(solution)/shard_map/reduce_scatter | solution.py:115
  190.0 1.9 copy-start.3
  191.9 1.0 copy-start.7
  281.5 110.8 %all-to-all-start.1 = ((bf16[32,1,128,1024]{3,2,1,0:T(8,128)(2,1)}), bf16[32,1,128,1024]{3,2,1,0:T(8,128)(2,1)}, u32[]{:S(2)}, u32[]{:S(2)}) async-start(bf16[32,1,128,1024]{3,2,1,0:T(8,128)(2,1)} %bitcast.120), calls=%async_computation.3 | async-start | bytes 16777216 | tf_op jit(solution)/shard_map/all_to_all | solution.py:147
  292.5 123.0 %all-gather.6.cloned.1.call-start = ((), (), s32[]{:S(2)}) async-start(), calls=%async_computation.8 | async-start | bytes 2621440 | tf_op jit(solution)/shard_map/all_gather | solution.py:168
  306.6 1.6 copy-start.12
  308.1 113.6 %all-gather.4.cloned.1.call-start = ((), (), s32[]{:S(2)}) async-start(), calls=%async_computation.6 | async-start | bytes 2621440 | tf_op jit(solution)/shard_map/all_gather | solution.py:108
  311.8 153.1 %reduce-scatter.8.cloned.1.call-start = ((), (), s32[]{:S(2)}) async-start(), calls=%async_computation.9 | async-start | bytes 5242880 | tf_op jit(solution)/shard_map/reduce_scatter | solution.py:156
  403.7 5.1 %copy-start.5 = (bf16[4096,512]{1,0:T(8,128)(2,1)S(1)}, bf16[4096,512]{1,0:T(8,128)(2,1)}, u32[]{:S(2)}) copy-start(bf16[4096,512]{1,0:T(8,128)(2,1)} %param.12) | copy-start | bytes 12582916
  408.7 2.4 copy-start.6
  421.7 43.2 %copy-start.1 = (bf16[512,1024]{1,0:T(8,128)(2,1)S(1)}, bf16[512,1024]{1,0:T(8,128)(2,1)}, u32[]{:S(2)}) copy-start(bf16[512,1024]{1,0:T(8,128)(2,1)} %param.10) | copy-start | bytes 3145732
Sparse Core Ops, SparseCore 0:
  14.4 32.8 reduce-scatter.3
  79.7 30.6 reduce-scatter.5
  308.2 31.8 all-gather.5
  342.2 30.8 all-gather.3
  415.6 49.2 reduce-scatter.7
where the time goes:
time: 481 us; the launch traced here: 472 us
  waiting for transfers between devices  205 us (43%)
  matrix products  99.3 us (21%)
  local copies, waits for them, and re-layouts  89.5 us (19%)
  blocking collectives  27 us (6%)
  other arithmetic  19.9 us (4%)
  starting transfers between devices  16.8 us (3%)
  between operations  14.4 us (3%)
    all_to_all x1, waiting for transfers between devices, body(): lax.all_to_all(sending, 'dp', split_axis=0, concat_axis=0, tiled=True)  80.2 us
    all_to_all x1, waiting for transfers between devices, body(): lax.all_to_all(outgoing, 'dp', split_axis=0, concat_axis=0, tiled=True)  61.5 us
    reduce_scatter x1, waiting for transfers between devices, body(): lax.psum_scatter((term_keys + jnp.einsum('rtk,dk->rtd', value_grad, value...  37 us
    unnamed x35, local copies, waits for them, and re-layouts  35.6 us
    all_gather x1, blocking collectives, body(): lax.all_gather(neighbours, 'dp', axis=0, tiled=True).reshape(n_dp, -1)  27 us
    reduce_scatter x1, waiting for transfers between devices, body(): lax.psum_scatter(partial_grad.astype(jnp.bfloat16), 'head', scatter_dimen...  25.9 us
    dot_general x1, matrix products, body(): jnp.einsum('chqm,cqhd->cmhd', grad_scores, query_block, preferred_element...  15.9 us
    dot_general x1, matrix products, body(): jnp.dot(assign, slot_grads, precision=lax.Precision.HIGHEST, preferred_el...  14.1 us
  transfers between devices with their start and end apart: 7, of which 4 were waited for; matrix products, arithmetic and copies ran while one was open for 20% of the time, Pallas kernels for 0%

commit v1 on v0

v1 whole, which is shorter than its diff:
```python
import functools

import jax
import jax.numpy as jnp
from jax import lax
from jax.experimental import pallas as pl
from jax.experimental.pallas import tpu as pltpu
from jax.sharding import PartitionSpec as P

HD = 128
SPAN = 64
NTOK = 128
MESH = pl.DeviceIdType.MESH
BF = jnp.bfloat16
F32 = jnp.float32
NEG = -1e30
SCALE = HD**-0.5
ANY = pl.BlockSpec(memory_space=pl.ANY)
VM = pl.BlockSpec(memory_space=pltpu.VMEM)
SM = pl.BlockSpec(memory_space=pltpu.SMEM)
CHUNKS = 4
TC = NTOK // CHUNKS


def dot(a, b, ca, cb):
    return lax.dot_general(a, b, (((ca,), (cb,)), ((), ())), preferred_element_type=F32)


class Ring:
    def __init__(self, me, place):
        self.me = me
        self.p = me + 1 - 2 * (me % 2)
        self.q = 3 - me
        self.far = (me + 2) % 4
        self.dev_p = place(self.p)
        self.dev_q = place(self.q)
        self.dev_far = place(self.far)


def rings():
    dp = lax.axis_index("dp")
    x = lax.axis_index("head")
    z, y, c = dp // 8, (dp // 2) % 4, dp % 2
    ring_z = Ring(z, lambda v: ((v * 4 + y) * 2 + c, x))
    ring_y = Ring(y, lambda v: ((z * 4 + v) * 2 + c, x))
    ring_x = Ring(x, lambda v: (dp, v))
    sister = ((z * 4 + y) * 2 + 1 - c, x)
    return ring_z, ring_y, ring_x, sister, c


def greet(devices):
    barrier = pltpu.get_barrier_semaphore()
    for device in devices:
        pl.semaphore_signal(barrier, inc=1, device_id=device, device_id_type=MESH)
    pl.semaphore_wait(barrier, len(devices))


class Copies:
    def __init__(self, send, recv, local):
        self.send, self.recv, self.local = send, recv, local
        self.remote_count = self.local_count = 0
        self.started = []

    def push(self, src, dst, device):
        index = self.remote_count
        self.remote_count += 1
        copy = pltpu.make_async_remote_copy(
            src_ref=src,
            dst_ref=dst,
            send_sem=self.send.at[index],
            recv_sem=self.recv.at[index],
            device_id=device,
            device_id_type=MESH,
        )
        copy.start()
        self.started.append(copy)
        return copy

    def move(self, src, dst):
        index = self.local_count
        self.local_count += 1
        copy = pltpu.make_async_copy(src, dst, self.local.at[index])
        copy.start()
        return copy

    def finish(self):
        for copy in self.started:
            copy.wait_send()


class Reduce:
    def __init__(self, copies, ring, part, tmp, got):
        self.copies, self.ring, self.part, self.tmp, self.got = copies, ring, part, tmp, got

    def start(self):
        r, part = self.ring, self.part
        self.to_far = (
            self.copies.push(part(r.far, 0), self.tmp(0), r.dev_p),
            self.copies.push(part(r.far, 1), self.tmp(1), r.dev_q),
        )
        self.near = (
            self.copies.push(part(r.p, 0), self.got(0), r.dev_p),
            self.copies.push(part(r.q, 1), self.got(3), r.dev_q),
        )

    def relay(self, add):
        r, part = self.ring, self.part
        self.to_far[0].wait_recv()
        add(part(r.q, 0), part(r.q, 0), self.tmp(0))
        first = self.copies.push(part(r.q, 0), self.got(2), r.dev_q)
        self.to_far[1].wait_recv()
        add(part(r.p, 1), part(r.p, 1), self.tmp(1))
        second = self.copies.push(part(r.p, 1), self.got(1), r.dev_p)
        self.near = self.near + (first, second)

    def end(self, add, own):
        for copy in self.near:
            copy.wait_recv()
        add(own(0), self.part(self.ring.me, 0), self.got(0), self.got(2))
        add(own(1), self.part(self.ring.me, 1), self.got(1), self.got(3))


class Gather:
    def __init__(self, copies, ring, slot):
        self.copies, self.ring, self.slot = copies, ring, slot

    def start(self, own):
        r = self.ring
        self.to_p = self.copies.push(own, self.slot(r.me), r.dev_p)
        self.to_q = self.copies.push(own, self.slot(r.me), r.dev_q)

    def relay_p(self):
        r = self.ring
        self.to_p.wait_recv()
        self.fwd_q = self.copies.push(self.slot(r.p, 0), self.slot(r.p, 0), r.dev_q)

    def relay_q(self):
        r = self.ring
        self.to_q.wait_recv()
        self.fwd_p = self.copies.push(self.slot(r.q, 1), self.slot(r.q, 1), r.dev_p)

    def relay(self):
        self.relay_p()
        self.relay_q()

    def end(self):
        self.fwd_q.wait_recv()
        self.fwd_p.wait_recv()


def add_rows(out, *terms):
    lead = out.shape[0]
    if len(out.shape) == 3:
        for index in range(lead):
            total = terms[0][index].astype(F32)
            for term in terms[1:]:
                total = total + term[index].astype(F32)
            out[index] = total.astype(out.dtype)
        return
    step = 32

    def block(i, carry):
        rows = pl.ds(pl.multiple_of(i * step, step), step)
        total = terms[0][rows].astype(F32)
        for term in terms[1:]:
            total = total + term[rows].astype(F32)
        out[rows] = total.astype(out.dtype)
        return carry

    lax.fori_loop(0, lead // step, block, 0)


def fetch_kernel(
    hid, wq, enc, wk, wv, gout, wo, ids,
    qg_out, rows_out, ids_out,
    v_hid, v_wq, v_enc, v_wk, v_wv, v_gout, v_wo, part, tmp, got, own, kv, send, recv, local,
):
    ring_z, ring_y, ring_x, sister, c = rings()
    copies = Copies(send, recv, local)
    loads = [
        copies.move(a, b)
        for a, b in (
            (hid, v_hid), (wq, v_wq), (enc, v_enc), (wk, v_wk), (wv, v_wv), (gout, v_gout), (wo, v_wo),
        )
    ]
    greet(
        [ring_x.dev_p, ring_x.dev_q, ring_y.dev_p, ring_y.dev_q, ring_z.dev_p, ring_z.dev_q, ring_z.dev_far, sister]
    )
    id_copies = [
        copies.push(ids, ids_out.at[ring_z.me], d) for d in (ring_z.dev_p, ring_z.dev_q, ring_z.dev_far)
    ]
    locals_left = [copies.move(ids, ids_out.at[ring_z.me])]

    def rows_of(unit, half):
        return pl.ds((unit % 2) * 256 + half * 128, 128)

    def unit_of(u):
        w = u // 2
        reduce = Reduce(
            copies,
            ring_x,
            lambda i, half: part.at[w, i, rows_of(u, half)],
            lambda half: tmp.at[u, half],
            lambda k: got.at[u, k],
        )

        def slot(i, half=None):
            rows = pl.ds((u % 2) * 256, 256) if half is None else rows_of(u, half)
            return qg_out.at[w, i, rows]

        return reduce, Gather(copies, ring_z, slot)

    units = [unit_of(u) for u in range(4)]

    def own_part(u):
        return lambda half: own.at[u // 2, rows_of(u, half)]

    def reduced(u):
        reduce, gather = units[u]
        reduce.end(add_rows, own_part(u))
        block = own.at[u // 2, pl.ds((u % 2) * 256, 256)]
        gather.start(block)
        locals_left.append(copies.move(block, gather.slot(ring_z.me)))

    loads[0].wait()
    loads[1].wait()

    def query_tile(g, carry):
        cols = pl.ds(pl.multiple_of(g * 512, 512), 512)
        part[0, g] = dot(v_hid[...], v_wq[:, cols], 1, 0).astype(BF)
        return carry

    lax.fori_loop(0, 4, query_tile, 0)
    units[0][0].start()
    units[1][0].start()

    streams = []
    loads[2].wait()
    for s, weight in ((0, v_wk), (1, v_wv)):
        loads[3 + s].wait()

        def row_tile(i, carry):
            rows = pl.ds(pl.multiple_of(i * 256, 256), 256)
            kv[s, rows] = dot(v_enc[rows, :], weight[...], 1, 0).astype(BF)
            return carry

        lax.fori_loop(0, 2, row_tile, 0)

        def slot(i, half=None, s=s):
            block = rows_out.at[i * 2 + c, s]
            return block if half is None else block.at[pl.ds((half + s) % 2 * 256, 256)]

        gather = Gather(copies, ring_y, slot)
        gather.start(kv.at[s])
        to_sister = [copies.push(kv.at[s], slot(ring_y.me), sister)]
        locals_left.append(copies.move(kv.at[s], slot(ring_y.me)))
        streams.append((gather, to_sister))

    units[0][0].relay(add_rows)
    loads[5].wait()
    loads[6].wait()

    def grad_tile(g, carry):
        rows = pl.ds(pl.multiple_of(g * 512, 512), 512)
        part[1, g] = dot(v_gout[...], v_wo[rows, :], 1, 1).astype(BF)
        return carry

    lax.fori_loop(0, 4, grad_tile, 0)
    units[2][0].start()
    reduced(0)
    units[1][0].relay(add_rows)
    units[3][0].start()
    reduced(1)
    units[0][1].relay()
    units[2][0].relay(add_rows)

    def forward(s):
        gather, to_sister = streams[s]
        gather.relay_p()
        to_sister.append(copies.push(gather.slot(ring_y.p), gather.slot(ring_y.p), sister))
        gather.relay_q()
        to_sister.append(copies.push(gather.slot(ring_y.q), gather.slot(ring_y.q), sister))

    forward(0)
    reduced(2)
    units[1][1].relay()
    units[3][0].relay(add_rows)
    forward(1)
    reduced(3)
    units[2][1].relay()
    for gather, to_sister in streams:
        gather.fwd_q.wait_recv()
        to_sister.append(copies.push(gather.slot(ring_y.far, 0), gather.slot(ring_y.far, 0), sister))
        gather.fwd_p.wait_recv()
        to_sister.append(copies.push(gather.slot(ring_y.far, 1), gather.slot(ring_y.far, 1), sister))
    units[3][1].relay()
    for _, gather in units:
        gather.end()
    for _, to_sister in streams:
        for copy in to_sister:
            copy.wait_recv()
    for copy in id_copies:
        copy.wait_recv()
    for copy in locals_left:
        copy.wait()
    copies.finish()


def fetch(hid, wq, enc, wk, wv, gout, wo, ids):
    return pl.pallas_call(
        fetch_kernel,
        out_shape=[
            jax.ShapeDtypeStruct((2, 4, 512, 512), BF),
            jax.ShapeDtypeStruct((8, 2, 512, 512), BF),
            jax.ShapeDtypeStruct((4, 8, 128), jnp.int32),
        ],
        in_specs=[ANY] * 8,
        out_specs=[ANY] * 3,
        scratch_shapes=[
            pltpu.VMEM((512, 1024), BF),
            pltpu.VMEM((1024, 2048), BF),
            pltpu.VMEM((512, 4096), BF),
            pltpu.VMEM((4096, 512), BF),
            pltpu.VMEM((4096, 512), BF),
            pltpu.VMEM((512, 1024), BF),
            pltpu.VMEM((2048, 1024), BF),
            pltpu.VMEM((2, 4, 512, 512), BF),
            pltpu.VMEM((4, 2, 128, 512), BF),
            pltpu.VMEM((4, 4, 128, 512), BF),
            pltpu.VMEM((2, 512, 512), BF),
            pltpu.VMEM((2, 512, 512), BF),
            pltpu.SemaphoreType.DMA((64,)),
            pltpu.SemaphoreType.DMA((64,)),
            pltpu.SemaphoreType.DMA((16,)),
        ],
        compiler_params=pltpu.CompilerParams(
            collective_id=0, has_side_effects=True, vmem_limit_bytes=52 << 20
        ),
        name="project_and_gather",
    )(hid, wq, enc, wk, wv, gout, wo, ids)


def slot_of(ids_ref, loc_ref, index, k):
    entry = ids_ref[index // 8, index % 8, k]
    stored = loc_ref[entry % 256]
    z = lax.axis_index("dp") // 8
    live = jnp.logical_and(entry >= 256, stored // 32 == z)
    return live, stored % 32


def two_heads(block):
    zero = jnp.zeros((SPAN, HD), BF)
    return jnp.concatenate(
        [
            jnp.concatenate([block[:, :HD], zero], axis=1),
            jnp.concatenate([zero, block[:, HD:]], axis=1),
        ],
        axis=0,
    )


def stats_kernel(ids_ref, loc_ref, qg_ref, rows_ref, stats_ref):
    stats_ref[0] = jnp.full((64, 128), NEG, F32)
    stats_ref[1] = jnp.zeros((64, 128), F32)
    stats_ref[2] = jnp.zeros((64, 128), F32)

    def span(i, carry):
        for k in range(2):
            live, row = slot_of(ids_ref, loc_ref, i, k)

            @pl.when(live)
            def _():
                for pair in range(2):
                    cols = pl.ds(pair * 256, 256)
                    key = rows_ref[row // 4, 0, row % 4, :, cols]
                    value = rows_ref[row // 4, 1, row % 4, :, cols]
                    s = dot(key, two_heads(qg_ref[0, i, :, cols]), 1, 1) * SCALE
                    gw = dot(value, two_heads(qg_ref[1, i, :, cols]), 1, 1)
                    line = pl.ds(i * 2 + pair, 1)
                    top = jnp.max(s, axis=0, keepdims=True)
                    old = stats_ref[0, line, :]
                    new = jnp.maximum(top, old)
                    e = jnp.exp(s - new)
                    fade = jnp.exp(old - new)
                    stats_ref[0, line, :] = new
                    stats_ref[1, line, :] = stats_ref[1, line, :] * fade + jnp.sum(e, axis=0, keepdims=True)
                    stats_ref[2, line, :] = stats_ref[2, line, :] * fade + jnp.sum(e * gw, axis=0, keepdims=True)

        return carry

    lax.fori_loop(0, 32, span, 0)


def stats_of(ids, loc, qg, rows):
    return pl.pallas_call(
        stats_kernel,
        out_shape=jax.ShapeDtypeStruct((3, 64, 128), F32),
        in_specs=[SM, SM, VM, VM],
        out_specs=VM,
        compiler_params=pltpu.CompilerParams(vmem_limit_bytes=52 << 20),
        name="span_stats",
    )(ids, loc, qg, rows)


def combine_kernel(stats_ref, out_ref, held, send, recv):
    ring_z, _, _, _, _ = rings()
    others = (ring_z.dev_p, ring_z.dev_q, ring_z.dev_far)
    greet(others)
    copies = Copies(send, recv, None)
    pushed = [copies.push(stats_ref, held.at[k], device) for k, device in enumerate(others)]
    for copy in pushed:
        copy.wait_recv()
    tops = [stats_ref[0]] + [held[k, 0] for k in range(3)]
    sums = [stats_ref[1]] + [held[k, 1] for k in range(3)]
    dots = [stats_ref[2]] + [held[k, 2] for k in range(3)]
    top = jnp.maximum(jnp.maximum(tops[0], tops[1]), jnp.maximum(tops[2], tops[3]))
    fades = [jnp.exp(t - top) for t in tops]
    total = sum(f * s for f, s in zip(fades, sums))
    inner = sum(f * d for f, d in zip(fades, dots))
    out_ref[0] = top
    out_ref[1] = 1.0 / total
    out_ref[2] = inner / total
    copies.finish()


def combine(stats):
    return pl.pallas_call(
        combine_kernel,
        out_shape=jax.ShapeDtypeStruct((3, 64, 128), F32),
        in_specs=[VM],
        out_specs=VM,
        scratch_shapes=[
            pltpu.VMEM((3, 3, 64, 128), F32),
            pltpu.SemaphoreType.DMA((3,)),
            pltpu.SemaphoreType.DMA((3,)),
        ],
        compiler_params=pltpu.CompilerParams(collective_id=1, has_side_effects=True),
        name="combine_stats",
    )(stats)


def attend_kernel(ids_ref, loc_ref, qg_ref, rows_ref, stats_ref, og_ref, grads_ref):
    def clear(i, carry):
        for s in range(2):
            for r in range(4):
                grads_ref[i, s, r] = jnp.zeros((NTOK, 512), BF)
        return carry

    lax.fori_loop(0, 8, clear, 0)

    def span(i, carry):
        og_ref[0, i] = jnp.zeros((SPAN, 512), BF)
        og_ref[1, i] = jnp.zeros((SPAN, 512), BF)
        for k in range(2):
            live, row = slot_of(ids_ref, loc_ref, i, k)

            @pl.when(live)
            def _():
                for pair in range(2):
                    cols = pl.ds(pair * 256, 256)
                    key = rows_ref[row // 4, 0, row % 4, :, cols]
                    value = rows_ref[row // 4, 1, row % 4, :, cols]
                    query = two_heads(qg_ref[0, i, :, cols])
                    grad = two_heads(qg_ref[1, i, :, cols])
                    line = pl.ds(i * 2 + pair, 1)
                    s = dot(key, query, 1, 1) * SCALE
                    gw = dot(value, grad, 1, 1)
                    w = jnp.exp(s - stats_ref[0, line, :]) * stats_ref[1, line, :]
                    ds = (w * (gw - stats_ref[2, line, :]) * SCALE).astype(BF)
                    w = w.astype(BF)
                    for which, probs, memory, other in ((0, w, value, grad), (1, ds, key, query)):
                        out = dot(probs, memory, 0, 0)
                        for h in range(2):
                            head = pl.ds(pair * 256 + h * HD, HD)
                            part = out[h * SPAN : (h + 1) * SPAN, h * HD : (h + 1) * HD]
                            og_ref[which, i, :, head] = (
                                og_ref[which, i, :, head].astype(F32) + part
                            ).astype(BF)
                        s_index = 1 - which
                        grads_ref[row // 4, s_index, row % 4, :, cols] = (
                            grads_ref[row // 4, s_index, row % 4, :, cols].astype(F32)
                            + dot(probs, other, 1, 0)
                        ).astype(BF)

        return carry

    lax.fori_loop(0, 32, span, 0)


def attend(ids, loc, qg, rows, stats):
    return pl.pallas_call(
        attend_kernel,
        out_shape=[
            jax.ShapeDtypeStruct((2, 32, SPAN, 512), BF),
            jax.ShapeDtypeStruct((8, 2, 4, NTOK, 512), BF),
        ],
        in_specs=[SM, SM, VM, VM, VM],
        out_specs=[VM, VM],
        compiler_params=pltpu.CompilerParams(vmem_limit_bytes=52 << 20),
        name="attend_both_ways",
    )(ids, loc, qg, rows, stats)


def return_kernel(
    og_part, grads, wk, wv, wo, wq,
    attended, grad_hidden, grad_encoded,
    v_wk, v_wv, v_wo, v_wq, og, z_tmp, z_got, own, everyone, rg, c_got, y_tmp, y_got, mine, term, x_tmp, x_got,
    send, recv, local,
):
    ring_z, ring_y, ring_x, sister, c = rings()
    copies = Copies(send, recv, local)
    og_loads = [copies.move(og_part.at[w], og.at[w]) for w in range(2)]
    order = (ring_y.far, ring_y.p, ring_y.q, ring_y.me)
    rg_loads = [
        [
            copies.move(grads.at[i * 2 + c, :, :, pl.ds(t * TC, TC)], rg.at[i, :, :, pl.ds(t * TC, TC)])
            for i in order
        ]
        for t in range(CHUNKS)
    ]
    weight_loads = [copies.move(a, b) for a, b in ((wk, v_wk), (wv, v_wv), (wo, v_wo), (wq, v_wq))]
    greet([ring_x.dev_p, ring_x.dev_q, ring_y.dev_p, ring_y.dev_q, ring_z.dev_p, ring_z.dev_q, sister])
    swaps = [
        [
            copies.push(
                grads.at[i * 2 + 1 - c, :, :, pl.ds(t * TC, TC)],
                c_got.at[i, :, :, pl.ds(t * TC, TC)],
                sister,
            )
            for i in order
        ]
        for t in range(CHUNKS)
    ]

    def rows_of(unit, half):
        return pl.ds((unit % 2) * 256 + half * 128, 128)

    def z_unit(u):
        w = u // 2
        reduce = Reduce(
            copies,
            ring_z,
            lambda i, half: og.at[w, i, rows_of(u, half)],
            lambda half: z_tmp.at[u, half],
            lambda k: z_got.at[u, k],
        )

        def slot(i, half=None):
            rows = pl.ds((u % 2) * 256, 256) if half is None else rows_of(u, half)
            return everyone.at[w, i, rows]

        return reduce, Gather(copies, ring_x, slot)

    def y_unit(t):
        rows = pl.ds(t * TC, TC)
        by_row = Reduce(
            copies,
            ring_y,
            lambda i, half: rg.at[i, half, :, rows],
            lambda half: y_tmp.at[half, :, rows],
            lambda k: y_got.at[k, :, rows],
        )
        by_group = Reduce(
            copies,
            ring_x,
            lambda i, half: term.at[i, rows, pl.ds(half * 2048, 2048)],
            lambda half: x_tmp.at[half, rows],
            lambda k: x_got.at[k, rows],
        )
        return by_row, by_group

    z_units = [z_unit(u) for u in range(4)]
    y_units = [y_unit(t) for t in range(CHUNKS)]

    def z_done(u):
        reduce, gather = z_units[u]
        reduce.end(add_rows, lambda half: own.at[u // 2, rows_of(u, half)])
        block = own.at[u // 2, pl.ds((u % 2) * 256, 256)]
        gather.start(block)
        everyone[u // 2, ring_x.me, pl.ds((u % 2) * 256, 256)] = block[...]

    def y_start(t):
        rows = pl.ds(t * TC, TC)
        for k, i in enumerate(order):
            rg_loads[t][k].wait()
            swaps[t][k].wait_recv()
            for half in range(2):
                block = rg.at[i, half, :, rows]
                add_rows(block, block, c_got.at[i, half, :, rows])
        y_units[t][0].start()

    def y_done(t):
        rows = pl.ds(t * TC, TC)
        y_units[t][0].end(add_rows, lambda half: mine.at[half, :, rows])
        if t == 0:
            weight_loads[0].wait()
            weight_loads[1].wait()

        def tile(j, carry):
            cols = pl.ds(pl.multiple_of(j * 512, 512), 512)
            keys = mine[0, :, rows, :].reshape(4 * TC, 512)
            values = mine[1, :, rows, :].reshape(4 * TC, 512)
            product = dot(keys, v_wk[cols, :], 1, 1) + dot(values, v_wv[cols, :], 1, 1)
            term[:, rows, cols] = product.astype(BF).reshape(4, TC, 512)
            return carry

        lax.fori_loop(0, 8, tile, 0)
        y_units[t][1].start()

    for w in range(2):
        og_loads[w].wait()
    z_units[0][0].start()
    y_start(0)
    z_units[1][0].start()
    y_start(1)
    for k in range(4):
        z_units[k][0].relay(add_rows)
        y_units[k][0].relay(add_rows)
        if k + 2 < 4:
            z_units[k + 2][0].start()
            y_start(k + 2)
        y_done(k)
        z_done(k)
        if k >= 1:
            y_units[k - 1][1].relay(add_rows)
            z_units[k - 1][1].relay()
    y_units[3][1].relay(add_rows)
    z_units[3][1].relay()

    weight_loads[2].wait()
    weight_loads[3].wait()

    def result(t):
        rows = pl.ds(t * TC, TC)
        y_units[t][1].end(add_rows, lambda half: grad_encoded.at[rows, pl.ds(half * 2048, 2048)])

    def attended_tile(i, carry):
        rows = pl.ds(pl.multiple_of(i * 128, 128), 128)
        total = dot(everyone[0, 0, rows, :], v_wo[0:512, :], 1, 0)
        for g in range(1, 4):
            total = total + dot(everyone[0, g, rows, :], v_wo[g * 512 : (g + 1) * 512, :], 1, 0)
        attended[rows, :] = total.astype(BF)
        return carry

    def hidden_tile(i, carry):
        rows = pl.ds(pl.multiple_of(i * 128, 128), 128)
        total = dot(everyone[1, 0, rows, :], v_wq[:, 0:512], 1, 1)
        for g in range(1, 4):
            total = total + dot(everyone[1, g, rows, :], v_wq[:, g * 512 : (g + 1) * 512], 1, 1)
        grad_hidden[rows, :] = total.astype(BF)
        return carry

    result(0)
    result(1)
    z_units[0][1].end()
    z_units[1][1].end()
    lax.fori_loop(0, 4, attended_tile, 0)
    result(2)
    result(3)
    z_units[2][1].end()
    z_units[3][1].end()
    lax.fori_loop(0, 4, hidden_tile, 0)
    copies.finish()


def give_back(og_part, grads, wk, wv, wo, wq):
    return pl.pallas_call(
        return_kernel,
        out_shape=[
            jax.ShapeDtypeStruct((512, 1024), BF),
            jax.ShapeDtypeStruct((512, 1024), BF),
            jax.ShapeDtypeStruct((NTOK, 4096), BF),
        ],
        in_specs=[ANY] * 6,
        out_specs=[VM] * 3,
        scratch_shapes=[
            pltpu.VMEM((4096, 512), BF),
            pltpu.VMEM((4096, 512), BF),
            pltpu.VMEM((2048, 1024), BF),
            pltpu.VMEM((1024, 2048), BF),
            pltpu.VMEM((2, 4, 512, 512), BF),
            pltpu.VMEM((4, 2, 128, 512), BF),
            pltpu.VMEM((4, 4, 128, 512), BF),
            pltpu.VMEM((2, 512, 512), BF),
            pltpu.VMEM((2, 4, 512, 512), BF),
            pltpu.VMEM((4, 2, 4, NTOK, 512), BF),
            pltpu.VMEM((4, 2, 4, NTOK, 512), BF),
            pltpu.VMEM((2, 4, NTOK, 512), BF),
            pltpu.VMEM((4, 4, NTOK, 512), BF),
            pltpu.VMEM((2, 4, NTOK, 512), BF),
            pltpu.VMEM((4, NTOK, 4096), BF),
            pltpu.VMEM((2, NTOK, 2048), BF),
            pltpu.VMEM((4, NTOK, 2048), BF),
            pltpu.SemaphoreType.DMA((112,)),
            pltpu.SemaphoreType.DMA((112,)),
            pltpu.SemaphoreType.DMA((32,)),
        ],
        compiler_params=pltpu.CompilerParams(
            collective_id=2, has_side_effects=True, vmem_limit_bytes=60 << 20
        ),
        name="reduce_and_project",
    )(og_part, grads, wk, wv, wo, wq)


def shift_up(rows):
    return jnp.pad(rows[SPAN - 1 :], ((0, SPAN - 1), (0, 0)))


def shift_down(rows):
    return jnp.pad(rows[: rows.shape[0] - SPAN + 1], ((SPAN - 1, 0), (0, 0)))


def body(
    hidden, query_weight, key_weight, value_weight, output_weight,
    encoded, location, neighbours, pattern, grad_out,
):
    ids = jnp.pad(neighbours + 256 * pattern, ((0, 0), (0, 126)))
    qg, rows, every_ids = fetch(
        shift_up(hidden), query_weight, encoded.reshape(512, 4096),
        key_weight, value_weight, shift_up(grad_out), output_weight, ids,
    )
    qg = qg.reshape(2, 32, SPAN, 512)
    rows = rows.reshape(8, 2, 4, NTOK, 512)
    stats = combine(stats_of(every_ids, location, qg, rows))
    og, grads = attend(every_ids, location, qg, rows, stats)
    attended, grad_hidden, grad_encoded = give_back(
        og.reshape(2, 4, 512, 512), grads, key_weight, value_weight, output_weight, query_weight
    )
    return shift_down(attended), shift_down(grad_hidden), grad_encoded.reshape(1, NTOK, 4096)


def solution(mesh):
    return jax.shard_map(
        body,
        mesh=mesh,
        in_specs=(
            P("dp", "head"),
            P("head", None),
            P(None, "head"),
            P(None, "head"),
            P(None, "head"),
            P("dp", None, None),
            P(),
            P("dp", None),
            P("dp", None),
            P("dp", "head"),
        ),
        out_specs=(P("dp", "head"), P("dp", "head"), P(("dp", "head"), None, None)),
        check_vma=False,
    )
```

time: 481 us -> 227 us (0.47)
  the two profiles are of different devices: /device:TPU:1 before, /device:TPU:2 now
where the time goes in v1:
time: 227 us
  Pallas kernels  216 us (95%)
  local copies, waits for them, and re-layouts  10.8 us (5%)
    pallas_call x1, Pallas kernels, give_back(): pl.pallas_call(return_kernel, out_shape=[jax.ShapeDtypeStruct((512, 1024)...  111 us
    pallas_call x1, Pallas kernels, fetch(): pl.pallas_call(fetch_kernel, out_shape=[jax.ShapeDtypeStruct((2, 4, 512,...  64.1 us
    pallas_call x1, Pallas kernels, attend(): pl.pallas_call(attend_kernel, out_shape=[jax.ShapeDtypeStruct((2, 32, SPA...  20.5 us
    pallas_call x1, Pallas kernels, stats_of(): pl.pallas_call(stats_kernel, out_shape=jax.ShapeDtypeStruct((3, 64, 128),...  9.95 us
    pallas_call x1, Pallas kernels, combine(): pl.pallas_call(combine_kernel, out_shape=jax.ShapeDtypeStruct((3, 64, 128...  9.63 us

profile of v1, /device:TPU:2, one launch (start us, length us, event | category | flops | bytes accessed | tf_op | source)
XLA Modules:
  0.0 227.1 jit_solution(14845973729468211798)
XLA Ops:
  0.6 0.0 copy-start.4
  0.6 0.8 copy.14
  1.5 0.8 copy.13
  2.3 1.4 slice.12
  3.7 0.1 pad.18.hid
  3.8 0.0 copy-done.4
  3.8 0.2 slice.13
  4.0 1.1 pad.19.gout
  5.1 0.0 copy-start.2
  5.1 64.1 %project_and_gather.1 = (bf16[2,4,512,512]{3,2,1,0:T(8,128)(2,1)}, bf16[8,2,512,512]{3,2,1,0:T(8,128)(2,1)}, s32[4,8,128]{2,1,0:T(8,128)S(1)}) custom-call(bf16[512,1024]{1,0:T(8,128)(2,1)S(1)} %pad.18.hid, bf16[1024,2048]{1,0:T(8,128)(2,1)} %wq.3, bf16[512,4096]{1,0:T(8,128)(2,1)} %bitcast.10, bf16[4096,512]{1,0:T(8,128)(2,1)} %wk.3, bf16[4096,512]{1,0:T(8,128)(2,1)} %wv.3, ...), custom_call_target="tpu_custom_call" | custom-call | tf_op jit(solution)/shard_map/project_and_gather/pallas_call | solution.py:310
  69.2 0.0 copy-done.2
  69.2 9.9 %span_stats.1.stats_ref = f32[3,64,128]{2,1,0:T(8,128)S(1)} custom-call(s32[4,8,128]{2,1,0:T(8,128)S(1)} %get-tuple-element.11.ids_ref, s32[128]{0:T(128)S(1)} %copy-done.2, bf16[2,32,64,512]{3,2,1,0:T(8,128)(2,1)} %bitcast.7, bf16[8,2,4,128,512]{4,3,2,1,0:T(8,128)(2,1)} %bitcast.5), custom_call_target="tpu_custom_call" | custom-call | tf_op jit(solution)/shard_map/span_stats/pallas_call | solution.py:395
  79.2 0.0 copy-start.1
  79.2 0.6 copy-done.1
  79.8 9.6 %combine_stats.1.stats_ref = f32[3,64,128]{2,1,0:T(8,128)} custom-call(f32[3,64,128]{2,1,0:T(8,128)} %copy-done.1), custom_call_target="tpu_custom_call" | custom-call | tf_op jit(solution)/shard_map/combine_stats/pallas_call | solution.py:427
  89.4 0.0 copy-start
  89.4 0.9 copy-done
  90.3 20.5 %attend_both_ways.1 = (bf16[2,32,64,512]{3,2,1,0:T(8,128)(2,1)}, bf16[8,2,4,128,512]{4,3,2,1,0:T(8,128)(2,1)}) custom-call(s32[4,8,128]{2,1,0:T(8,128)S(1)} %get-tuple-element.11.ids_ref, s32[128]{0:T(128)S(1)} %copy-done.2, bf16[2,32,64,512]{3,2,1,0:T(8,128)(2,1)} %bitcast.8, bf16[8,2,4,128,512]{4,3,2,1,0:T(8,128)(2,1)} %bitcast.6, f32[3,64,128]{2,1,0:T(8,128)S(1)} %copy-done), custom_call_target="tpu_custom_call" | custom-call | tf_op jit(solution)/shard_map/attend_both_ways/pallas_call | solution.py:491
  110.8 111.4 %reduce_and_project.1 = (bf16[512,1024]{1,0:T(8,128)(2,1)}, bf16[512,1024]{1,0:T(8,128)(2,1)}, bf16[128,4096]{1,0:T(8,128)(2,1)}) custom-call(bf16[2,4,512,512]{3,2,1,0:T(8,128)(2,1)} %bitcast.9, bf16[8,2,4,128,512]{4,3,2,1,0:T(8,128)(2,1)} %get-tuple-element.15.grads, bf16[4096,512]{1,0:T(8,128)(2,1)} %wk.3, bf16[4096,512]{1,0:T(8,128)(2,1)} %wv.3, ...), custom_call_target="tpu_custom_call" | custom-call | tf_op jit(solution)/shard_map/reduce_and_project/pallas_call | solution.py:667
  222.2 0.0 copy-start.5
  222.2 0.0 copy-start.3
  222.2 1.4 slice.14
  223.6 1.2 pad.21
  224.8 0.0 copy-done.5
  224.8 0.1 slice.15
  224.9 1.2 pad.22
  226.1 0.0 copy-done.3
  226.1 1.0 copy.16
  (2 shorter events, 0.0 us)
Async XLA Ops:
  0.6 3.2 %copy-start.4 = (bf16[512,1024]{1,0:T(8,128)(2,1)S(1)}, bf16[512,1024]{1,0:T(8,128)(2,1)}, u32[]{:S(2)}) copy-start(bf16[512,1024]{1,0:T(8,128)(2,1)} %param.19) | copy-start | bytes 3145732
  5.1 64.1 %copy-start.2 = (s32[128]{0:T(128)S(1)}, s32[128]{0:T(128)}, u32[]{:S(2)}) copy-start(s32[128]{0:T(128)} %loc_ref.3) | copy-start | bytes 1540
  79.2 0.6 copy-start.1
  89.4 0.9 copy-start
  222.2 2.6 %copy-start.5 = (bf16[512,1024]{1,0:T(8,128)(2,1)S(1)}, bf16[512,1024]{1,0:T(8,128)(2,1)}, u32[]{:S(2)}) copy-start(bf16[512,1024]{1,0:T(8,128)(2,1)} %get-tuple-element.17) | copy-start | bytes 3145732
  222.2 3.9 %copy-start.3 = (bf16[128,4096]{1,0:T(8,128)(2,1)S(1)}, bf16[128,4096]{1,0:T(8,128)(2,1)}, u32[]{:S(2)}) copy-start(bf16[128,4096]{1,0:T(8,128)(2,1)} %get-tuple-element.18) | copy-start | bytes 3145732

commit v2 on v1

v2 whole, which is shorter than its diff:
```python
import functools

import jax
import jax.numpy as jnp
from jax import lax
from jax.experimental import pallas as pl
from jax.experimental.pallas import tpu as pltpu
from jax.sharding import PartitionSpec as P

HD = 128
SPAN = 64
NTOK = 128
MESH = pl.DeviceIdType.MESH
BF = jnp.bfloat16
F32 = jnp.float32
NEG = -1e30
SCALE = HD**-0.5
ANY = pl.BlockSpec(memory_space=pl.ANY)
VM = pl.BlockSpec(memory_space=pltpu.VMEM)
SM = pl.BlockSpec(memory_space=pltpu.SMEM)
CHUNKS = 4
TC = NTOK // CHUNKS
OUTPUT_UNITS = ((0, 0, 128), (0, 128, 128), (0, 256, 256), (1, 0, 256), (1, 256, 256))
QUERY_UNITS = tuple((w, first, 128) for w in range(2) for first in range(0, 512, 128))


def dot(a, b, ca, cb):
    return lax.dot_general(a, b, (((ca,), (cb,)), ((), ())), preferred_element_type=F32)


class Ring:
    def __init__(self, me, place):
        self.me = me
        self.p = me + 1 - 2 * (me % 2)
        self.q = 3 - me
        self.far = (me + 2) % 4
        self.dev_p = place(self.p)
        self.dev_q = place(self.q)
        self.dev_far = place(self.far)


def rings():
    dp = lax.axis_index("dp")
    x = lax.axis_index("head")
    z, y, c = dp // 8, (dp // 2) % 4, dp % 2
    ring_z = Ring(z, lambda v: ((v * 4 + y) * 2 + c, x))
    ring_y = Ring(y, lambda v: ((z * 4 + v) * 2 + c, x))
    ring_x = Ring(x, lambda v: (dp, v))
    sister = ((z * 4 + y) * 2 + 1 - c, x)
    return ring_z, ring_y, ring_x, sister, c


def greet(devices):
    barrier = pltpu.get_barrier_semaphore()
    for device in devices:
        pl.semaphore_signal(barrier, inc=1, device_id=device, device_id_type=MESH)
    pl.semaphore_wait(barrier, len(devices))


class Copies:
    def __init__(self, send, recv, local):
        self.send, self.recv, self.local = send, recv, local
        self.remote_count = self.local_count = 0
        self.started = []

    def push(self, src, dst, device):
        index = self.remote_count
        self.remote_count += 1
        copy = pltpu.make_async_remote_copy(
            src_ref=src,
            dst_ref=dst,
            send_sem=self.send.at[index],
            recv_sem=self.recv.at[index],
            device_id=device,
            device_id_type=MESH,
        )
        copy.start()
        self.started.append(copy)
        return copy

    def move(self, src, dst):
        index = self.local_count
        self.local_count += 1
        copy = pltpu.make_async_copy(src, dst, self.local.at[index])
        copy.start()
        return copy

    def finish(self):
        for copy in self.started:
            copy.wait_send()


class Reduce:
    def __init__(self, copies, ring, part, tmp, got):
        self.copies, self.ring, self.part, self.tmp, self.got = copies, ring, part, tmp, got

    def start(self):
        r, part = self.ring, self.part
        self.to_far = (
            self.copies.push(part(r.far, 0), self.tmp(0), r.dev_p),
            self.copies.push(part(r.far, 1), self.tmp(1), r.dev_q),
        )
        self.near = (
            self.copies.push(part(r.p, 0), self.got(0), r.dev_p),
            self.copies.push(part(r.q, 1), self.got(3), r.dev_q),
        )

    def relay(self, add):
        r, part = self.ring, self.part
        self.to_far[0].wait_recv()
        add(part(r.q, 0), part(r.q, 0), self.tmp(0))
        first = self.copies.push(part(r.q, 0), self.got(2), r.dev_q)
        self.to_far[1].wait_recv()
        add(part(r.p, 1), part(r.p, 1), self.tmp(1))
        second = self.copies.push(part(r.p, 1), self.got(1), r.dev_p)
        self.near = self.near + (first, second)

    def end(self, add, own):
        for copy in self.near:
            copy.wait_recv()
        add(own(0), self.part(self.ring.me, 0), self.got(0), self.got(2))
        add(own(1), self.part(self.ring.me, 1), self.got(1), self.got(3))


class Gather:
    def __init__(self, copies, ring, slot):
        self.copies, self.ring, self.slot = copies, ring, slot

    def start(self, own):
        r = self.ring
        self.to_p = self.copies.push(own, self.slot(r.me), r.dev_p)
        self.to_q = self.copies.push(own, self.slot(r.me), r.dev_q)

    def relay_p(self):
        r = self.ring
        self.to_p.wait_recv()
        self.fwd_q = self.copies.push(self.slot(r.p, 0), self.slot(r.p, 0), r.dev_q)

    def relay_q(self):
        r = self.ring
        self.to_q.wait_recv()
        self.fwd_p = self.copies.push(self.slot(r.q, 1), self.slot(r.q, 1), r.dev_p)

    def relay(self):
        self.relay_p()
        self.relay_q()

    def end(self):
        self.fwd_q.wait_recv()
        self.fwd_p.wait_recv()


def add_up(terms):
    if len(terms) == 2:
        return terms[0] + terms[1]
    return sum(t.astype(F32) for t in terms).astype(BF)


def add_rows(out, *terms):
    if len(out.shape) == 3:
        for index in range(out.shape[0]):
            out[index] = add_up([t[index] for t in terms])
        return

    def block(i, carry):
        rows = pl.ds(pl.multiple_of(i * 32, 32), 32)
        out[rows] = add_up([t[rows] for t in terms])
        return carry

    lax.fori_loop(0, out.shape[0] // 32, block, 0)


def fetch_kernel(
    loc_ref, hid, wq, enc, wk, wv, gout, wo, ids,
    qg_out, rows_out, ids_out, stats_out,
    v_hid, v_wq, v_enc, v_wk, v_wv, v_gout, v_wo, part, tmp, got, shifted, qg, rows, ids_ref, stats, held,
    send, recv, local,
):
    ring_z, ring_y, ring_x, sister, c = rings()
    copies = Copies(send, recv, local)
    loads = [
        copies.move(a, b)
        for a, b in (
            (hid, v_hid), (wq, v_wq), (enc, v_enc), (wk, v_wk), (wv, v_wv), (gout, v_gout), (wo, v_wo),
        )
    ]
    greet(
        [ring_x.dev_p, ring_x.dev_q, ring_y.dev_p, ring_y.dev_q, ring_z.dev_p, ring_z.dev_q, ring_z.dev_far, sister]
    )
    id_copies = [
        copies.push(ids, ids_out.at[ring_z.me], d) for d in (ring_z.dev_p, ring_z.dev_q, ring_z.dev_far)
    ]
    own_ids = copies.move(ids, ids_out.at[ring_z.me])

    def unit_of(u):
        w, first, size = QUERY_UNITS[u]
        half_size = size // 2

        def rows_of(half):
            return pl.ds(first + half * half_size, half_size)

        reduce = Reduce(
            copies,
            ring_x,
            lambda i, half: part.at[w, i, rows_of(half)],
            lambda half: tmp.at[w, rows_of(half)],
            lambda k: got.at[w, k // 2, rows_of(k % 2)],
        )

        def slot(i, half=None):
            return qg.at[w, i, pl.ds(first, size) if half is None else rows_of(half)]

        return reduce, Gather(copies, ring_z, slot)

    units = [unit_of(u) for u in range(len(QUERY_UNITS))]

    def shift_tile(ref, t):
        first = min(t, 2) * 128
        row = lax.broadcasted_iota(jnp.int32, (128, 256), 0) + (t * 128 + SPAN - 1 - first)
        col = lax.broadcasted_iota(jnp.int32, (128, 256), 1)
        move = (row == col).astype(BF)
        shifted[pl.ds(t * 128, 128), :] = dot(move, ref[pl.ds(first, 256), :], 1, 0).astype(BF)

    def query_rows(first, size):
        def tile(g, carry):
            cols = pl.ds(pl.multiple_of(g * 512, 512), 512)
            here = pl.ds(first, size)
            part[0, g, here] = dot(shifted[here, :], v_wq[:, cols], 1, 0).astype(BF)
            return carry

        lax.fori_loop(0, 4, tile, 0)

    def begin(u):
        units[u][0].start()

    def relay(u):
        units[u][0].relay(add_rows)

    def reduced(u):
        reduce, gather = units[u]
        reduce.end(add_rows, lambda half: gather.slot(ring_z.me, half))
        gather.start(gather.slot(ring_z.me))

    def spread(u):
        units[u][1].relay()

    out_copies = []

    def complete(u):
        w, first, size = QUERY_UNITS[u]
        units[u][1].end()
        here = pl.ds(first, size)
        out_copies.append(copies.move(qg.at[w, :, here], qg_out.at[w, :, here]))

    streams = []

    def project(s, weight):
        mine = rows.at[ring_y.me * 2 + c, s]

        def tile(j, carry):
            cols = pl.ds(pl.multiple_of(j * 256, 256), 256)
            mine[:, :, cols] = dot(v_enc[...], weight[:, cols], 1, 0).astype(BF).reshape(4, NTOK, 256)
            return carry

        lax.fori_loop(0, 2, tile, 0)

        def slot(i, half=None):
            block = rows.at[i * 2 + c, s]
            return block if half is None else block.at[pl.ds((half + s) % 2 * 2, 2)]

        gather = Gather(copies, ring_y, slot)
        gather.start(mine)
        streams.append((gather, [copies.push(mine, mine, sister)]))

    def forward(s):
        gather, to_sister = streams[s]
        gather.relay_p()
        to_sister.append(copies.push(gather.slot(ring_y.p), gather.slot(ring_y.p), sister))
        gather.relay_q()
        to_sister.append(copies.push(gather.slot(ring_y.q), gather.slot(ring_y.q), sister))

    def forwarded(s):
        gather, to_sister = streams[s]
        gather.fwd_q.wait_recv()
        to_sister.append(copies.push(gather.slot(ring_y.far, 0), gather.slot(ring_y.far, 0), sister))
        gather.fwd_p.wait_recv()
        to_sister.append(copies.push(gather.slot(ring_y.far, 1), gather.slot(ring_y.far, 1), sister))

    def rows_complete(s):
        for copy in streams[s][1]:
            copy.wait_recv()
        out_copies.append(copies.move(rows.at[:, s], rows_out.at[:, s]))

    loads[0].wait()
    shift_tile(v_hid, 0)
    loads[1].wait()
    query_rows(0, 128)
    begin(0)
    for t in range(1, 4):
        shift_tile(v_hid, t)
    query_rows(128, 384)
    begin(1)
    relay(0)
    begin(2)
    loads[2].wait()
    loads[3].wait()
    project(0, v_wk)
    relay(1)
    begin(3)
    reduced(0)
    loads[4].wait()
    project(1, v_wv)
    relay(2)
    reduced(1)
    loads[5].wait()
    for t in range(4):
        shift_tile(v_gout, t)
    loads[6].wait()

    def grad_tile(g, carry):
        here = pl.ds(pl.multiple_of(g * 512, 512), 512)
        part[1, g] = dot(shifted[...], v_wo[here, :], 1, 1).astype(BF)
        return carry

    lax.fori_loop(0, 4, grad_tile, 0)
    begin(4)
    relay(3)
    begin(5)
    reduced(2)
    spread(0)
    relay(4)
    begin(6)
    reduced(3)
    spread(1)
    forward(0)
    relay(5)
    begin(7)
    reduced(4)
    spread(2)
    relay(6)
    reduced(5)
    spread(3)
    forward(1)
    for copy in id_copies:
        copy.wait_recv()
    own_ids.wait()
    copies.move(ids_out, ids_ref).wait()
    relay(7)
    reduced(6)
    spread(4)
    reduced(7)
    spread(5)
    forwarded(0)
    spread(6)
    forwarded(1)
    spread(7)
    for u in range(4):
        complete(u)
    rows_complete(0)
    rows_complete(1)
    plane = lax.axis_index("dp") // 8

    def stats_of_spans(first, n):
        def span(j, carry):
            i = j // n * 8 + first + j % n
            for pair in range(2):
                cols = pl.ds(pair * 256, 256)
                tokens = pl.ds(pl.multiple_of(i % 8 * SPAN, SPAN), SPAN)
                query = two_heads(qg[0, i // 8, tokens, cols])
                grad = two_heads(qg[1, i // 8, tokens, cols])
                made = []
                for k in range(2):
                    entry = ids_ref[i // 8, i % 8, k]
                    stored = loc_ref[entry % 256]
                    live = jnp.logical_and(entry >= 256, stored // 32 == plane).astype(F32)
                    row = stored % 32
                    key = rows[row // 4, 0, row % 4, :, cols]
                    value = rows[row // 4, 1, row % 4, :, cols]
                    score = dot(key, query, 1, 1) * SCALE
                    gw = dot(value, grad, 1, 1)
                    top = jnp.max(score, axis=0, keepdims=True)
                    e = jnp.exp(score - top)
                    total = jnp.sum(e, axis=0, keepdims=True) * live
                    inner = jnp.sum(e * gw, axis=0, keepdims=True) * live
                    made.append((top * live + NEG * (1.0 - live), total, inner))
                (top0, sum0, dot0), (top1, sum1, dot1) = made
                top = jnp.maximum(top0, top1)
                f0, f1 = jnp.exp(top0 - top), jnp.exp(top1 - top)
                line = pl.ds(i * 2 + pair, 1)
                stats[0, line, :] = top
                stats[1, line, :] = sum0 * f0 + sum1 * f1
                stats[2, line, :] = dot0 * f0 + dot1 * f1
            return carry

        lax.fori_loop(0, 4 * n, span, 0)

    for u in range(4):
        complete(4 + u)
        stats_of_spans(2 * u, 2)

    def stats_slot(i, half=None):
        return held.at[i] if half is None else held.at[i, :, pl.ds(half * 32, 32)]

    exchange = Gather(copies, ring_z, stats_slot)
    exchange.start(stats)
    held[ring_z.me] = stats[...]
    exchange.relay()
    exchange.end()
    tops = [held[k, 0] for k in range(4)]
    top = jnp.maximum(jnp.maximum(tops[0], tops[1]), jnp.maximum(tops[2], tops[3]))
    fades = [jnp.exp(t - top) for t in tops]
    total = sum(fades[k] * held[k, 1] for k in range(4))
    inner = sum(fades[k] * held[k, 2] for k in range(4))
    stats_out[0] = top
    stats_out[1] = 1.0 / total
    stats_out[2] = inner / total
    for copy in out_copies:
        copy.wait()
    copies.finish()


def fetch(loc, hid, wq, enc, wk, wv, gout, wo, ids):
    return pl.pallas_call(
        fetch_kernel,
        out_shape=[
            jax.ShapeDtypeStruct((2, 4, 512, 512), BF),
            jax.ShapeDtypeStruct((8, 2, 4, NTOK, 512), BF),
            jax.ShapeDtypeStruct((4, 8, 128), jnp.int32),
            jax.ShapeDtypeStruct((3, 64, 128), F32),
        ],
        in_specs=[SM] + [ANY] * 8,
        out_specs=[ANY] * 3 + [VM],
        scratch_shapes=[
            pltpu.VMEM((512, 1024), BF),
            pltpu.VMEM((1024, 2048), BF),
            pltpu.VMEM((512, 4096), BF),
            pltpu.VMEM((4096, 512), BF),
            pltpu.VMEM((4096, 512), BF),
            pltpu.VMEM((512, 1024), BF),
            pltpu.VMEM((2048, 1024), BF),
            pltpu.VMEM((2, 4, 512, 512), BF),
            pltpu.VMEM((2, 512, 512), BF),
            pltpu.VMEM((2, 2, 512, 512), BF),
            pltpu.VMEM((512, 1024), BF),
            pltpu.VMEM((2, 4, 512, 512), BF),
            pltpu.VMEM((8, 2, 4, NTOK, 512), BF),
            pltpu.SMEM((4, 8, 128), jnp.int32),
            pltpu.VMEM((3, 64, 128), F32),
            pltpu.VMEM((4, 3, 64, 128), F32),
            pltpu.SemaphoreType.DMA((112,)),
            pltpu.SemaphoreType.DMA((112,)),
            pltpu.SemaphoreType.DMA((32,)),
        ],
        compiler_params=pltpu.CompilerParams(
            collective_id=0, has_side_effects=True, vmem_limit_bytes=54 << 20
        ),
        name="project_and_gather",
    )(loc, hid, wq, enc, wk, wv, gout, wo, ids)


def list_live(ids_ref, loc_ref, live_ref):
    z = lax.axis_index("dp") // 8

    def one(i, count):
        entry = ids_ref[i // 16, (i // 2) % 8, i % 2]
        stored = loc_ref[entry % 256]
        live_ref[count] = (i // 2) * 32 + stored % 32
        live = jnp.logical_and(entry >= 256, stored // 32 == z)
        return count + live.astype(jnp.int32)

    return lax.fori_loop(0, 64, one, 0)


def pairs_of_slots(live_ref, count, work):
    def step(j, carry):
        first = live_ref[2 * j]
        both = 2 * j + 1 < count
        second = jnp.where(both, live_ref[2 * j + 1], first)
        work(
            (first // 32, first % 32, None),
            (second // 32, second % 32, both.astype(F32)),
        )
        return carry

    lax.fori_loop(0, (count + 1) // 2, step, 0)


def load_inputs(qg_ref, rows_ref, qg, rows, sems):
    moves = [pltpu.make_async_copy(qg_ref.at[w], qg.at[w], sems.at[w]) for w in range(2)]
    moves += [pltpu.make_async_copy(rows_ref.at[b], rows.at[b], sems.at[2 + b]) for b in range(8)]
    for move in moves:
        move.start()
    return moves


def two_heads(block):
    zero = jnp.zeros((SPAN, HD), BF)
    return jnp.concatenate(
        [
            jnp.concatenate([block[:, :HD], zero], axis=1),
            jnp.concatenate([zero, block[:, HD:]], axis=1),
        ],
        axis=0,
    )


LOCAL_SCRATCH = [
    pltpu.VMEM((2, 32, SPAN, 512), BF),
    pltpu.VMEM((8, 2, 4, NTOK, 512), BF),
    pltpu.SemaphoreType.DMA((10,)),
    pltpu.SMEM((65,), jnp.int32),
]


def attend_kernel(ids_ref, loc_ref, qg_ref, rows_ref, stats_ref, og_ref, grads_ref, qg, rows, sems, live_ref):
    moves = load_inputs(qg_ref, rows_ref, qg, rows, sems)
    count = list_live(ids_ref, loc_ref, live_ref)

    def clear(i, carry):
        for s in range(2):
            for r in range(4):
                grads_ref[i, s, r] = jnp.zeros((NTOK, 512), BF)
                og_ref[s, i * 4 + r] = jnp.zeros((SPAN, 512), BF)
        return carry

    lax.fori_loop(0, 8, clear, 0)
    for move in moves:
        move.wait()

    def work(*slots):
        made = []
        for i, row, weight in slots:
            for pair in range(2):
                cols = pl.ds(pair * 256, 256)
                key = rows[row // 4, 0, row % 4, :, cols]
                value = rows[row // 4, 1, row % 4, :, cols]
                query = two_heads(qg[0, i, :, cols])
                grad = two_heads(qg[1, i, :, cols])
                line = pl.ds(i * 2 + pair, 1)
                s = dot(key, query, 1, 1) * SCALE
                gw = dot(value, grad, 1, 1)
                share = stats_ref[1, line, :]
                if weight is not None:
                    share = share * weight
                w = jnp.exp(s - stats_ref[0, line, :]) * share
                ds = (w * (gw - stats_ref[2, line, :]) * SCALE).astype(BF)
                w = w.astype(BF)
                for which, probs, memory, other in ((0, w, value, grad), (1, ds, key, query)):
                    made.append((i, row, pair, which, dot(probs, memory, 0, 0), dot(probs, other, 1, 0)))
        for i, row, pair, which, out, slope in made:
            for h in range(2):
                head = pl.ds(pair * 256 + h * HD, HD)
                part = out[h * SPAN : (h + 1) * SPAN, h * HD : (h + 1) * HD]
                og_ref[which, i, :, head] = (og_ref[which, i, :, head].astype(F32) + part).astype(BF)
            cols = pl.ds(pair * 256, 256)
            grads_ref[row // 4, 1 - which, row % 4, :, cols] = (
                grads_ref[row // 4, 1 - which, row % 4, :, cols].astype(F32) + slope
            ).astype(BF)

    pairs_of_slots(live_ref, count, work)


def attend(ids, loc, qg, rows, stats):
    return pl.pallas_call(
        attend_kernel,
        out_shape=[
            jax.ShapeDtypeStruct((2, 32, SPAN, 512), BF),
            jax.ShapeDtypeStruct((8, 2, 4, NTOK, 512), BF),
        ],
        in_specs=[SM, SM, ANY, ANY, VM],
        out_specs=[VM, VM],
        scratch_shapes=LOCAL_SCRATCH,
        compiler_params=pltpu.CompilerParams(vmem_limit_bytes=52 << 20),
        name="attend_both_ways",
    )(ids, loc, qg, rows, stats)


def return_kernel(
    og_part, grads, wk, wv, wo, wq,
    attended, grad_hidden, grad_encoded,
    v_wk, v_wv, v_wo, v_wq, og, z_tmp, z_got, own, everyone, rg, c_got, y_tmp, y_got, mine, term, x_tmp, x_got,
    send, recv, local,
):
    ring_z, ring_y, ring_x, sister, c = rings()
    copies = Copies(send, recv, local)
    og_loads = [copies.move(og_part.at[w], og.at[w]) for w in range(2)]
    order = (ring_y.far, ring_y.p, ring_y.q, ring_y.me)
    rg_loads = [
        [
            copies.move(grads.at[i * 2 + c, :, :, pl.ds(t * TC, TC)], rg.at[i, :, :, pl.ds(t * TC, TC)])
            for i in order
        ]
        for t in range(CHUNKS)
    ]
    weight_loads = [copies.move(a, b) for a, b in ((wk, v_wk), (wv, v_wv), (wo, v_wo), (wq, v_wq))]
    greet([ring_x.dev_p, ring_x.dev_q, ring_y.dev_p, ring_y.dev_q, ring_z.dev_p, ring_z.dev_q, sister])
    swaps = [
        [
            copies.push(
                grads.at[i * 2 + 1 - c, :, :, pl.ds(t * TC, TC)],
                c_got.at[i, :, :, pl.ds(t * TC, TC)],
                sister,
            )
            for i in order
        ]
        for t in range(CHUNKS)
    ]

    def z_unit(u):
        w, first, size = OUTPUT_UNITS[u]
        half_size = size // 2

        def rows_of(half):
            return pl.ds(first + half * half_size, half_size)

        whole = pl.ds(first, size)
        reduce = Reduce(
            copies,
            ring_z,
            lambda i, half: og.at[w, i, rows_of(half)],
            lambda half: z_tmp.at[w, rows_of(half)],
            lambda k: z_got.at[w, k // 2, rows_of(k % 2)],
        )
        gather = Gather(
            copies, ring_x, lambda i, half=None: everyone.at[w, i, whole if half is None else rows_of(half)]
        )

        def done():
            reduce.end(add_rows, lambda half: own.at[w, rows_of(half)])
            gather.start(own.at[w, whole])
            everyone[w, ring_x.me, whole] = own[w, whole]

        return reduce, gather, done

    def y_unit(t):
        rows = pl.ds(t * TC, TC)
        by_row = Reduce(
            copies,
            ring_y,
            lambda i, half: rg.at[i, half, :, rows],
            lambda half: y_tmp.at[half, :, rows],
            lambda k: y_got.at[k, :, rows],
        )
        by_group = Reduce(
            copies,
            ring_x,
            lambda i, half: term.at[i, rows, pl.ds(half * 2048, 2048)],
            lambda half: x_tmp.at[half, rows],
            lambda k: x_got.at[k, rows],
        )
        return by_row, by_group

    z_units = [z_unit(u) for u in range(len(OUTPUT_UNITS))]
    y_units = [y_unit(t) for t in range(CHUNKS)]

    def y_start(t):
        rows = pl.ds(t * TC, TC)
        for k, i in enumerate(order):
            rg_loads[t][k].wait()
            swaps[t][k].wait_recv()
            for half in range(2):
                block = rg.at[i, half, :, rows]
                add_rows(block, block, c_got.at[i, half, :, rows])
        y_units[t][0].start()

    def y_done(t):
        rows = pl.ds(t * TC, TC)
        y_units[t][0].end(add_rows, lambda half: mine.at[half, :, rows])
        if t == 0:
            weight_loads[0].wait()
            weight_loads[1].wait()

        def tile(j, carry):
            cols = pl.ds(pl.multiple_of(j * 512, 512), 512)
            keys = mine[0, :, rows, :].reshape(4 * TC, 512)
            values = mine[1, :, rows, :].reshape(4 * TC, 512)
            product = dot(keys, v_wk[cols, :], 1, 1) + dot(values, v_wv[cols, :], 1, 1)
            term[:, rows, cols] = product.astype(BF).reshape(4, TC, 512)
            return carry

        lax.fori_loop(0, 8, tile, 0)
        y_units[t][1].start()

    def z_begin(u):
        z_units[u][0].start()

    def z_relay(u):
        z_units[u][0].relay(add_rows)

    def z_done(u):
        z_units[u][2]()

    def spread(u):
        z_units[u][1].relay()

    def y_relay(t):
        y_units[t][0].relay(add_rows)

    def x_relay(t):
        y_units[t][1].relay(add_rows)

    og_loads[0].wait()
    z_begin(0)
    z_begin(1)
    z_relay(0)
    y_start(0)
    z_begin(2)
    z_done(0)
    z_relay(1)
    y_start(1)
    y_relay(0)
    og_loads[1].wait()
    z_begin(3)
    z_done(1)
    spread(0)
    y_done(0)
    z_relay(2)
    y_start(2)
    y_relay(1)
    spread(1)
    z_done(2)
    z_begin(4)
    x_relay(0)
    y_done(1)
    z_relay(3)
    y_start(3)
    y_relay(2)
    spread(2)
    z_done(3)
    x_relay(1)
    y_done(2)
    z_relay(4)
    y_relay(3)
    spread(3)
    z_done(4)
    x_relay(2)
    y_done(3)
    spread(4)
    x_relay(3)

    weight_loads[2].wait()
    weight_loads[3].wait()

    def result(t):
        rows = pl.ds(t * TC, TC)
        y_units[t][1].end(add_rows, lambda half: grad_encoded.at[rows, pl.ds(half * 2048, 2048)])

    def attended_tile(j, carry):
        cols = pl.ds(pl.multiple_of(j * 256, 256), 256)
        total = dot(everyone[0, 0], v_wo[0:512, cols], 1, 0)
        for g in range(1, 4):
            total = total + dot(everyone[0, g], v_wo[g * 512 : (g + 1) * 512, cols], 1, 0)
        attended[:, cols] = total.astype(BF)
        return carry

    def hidden_rows(first):
        rows = pl.ds(first, 256)

        def tile(j, carry):
            cols = pl.ds(pl.multiple_of(j * 256, 256), 256)
            total = dot(everyone[1, 0, rows], v_wq[cols, 0:512], 1, 1)
            for g in range(1, 4):
                total = total + dot(everyone[1, g, rows], v_wq[cols, g * 512 : (g + 1) * 512], 1, 1)
            grad_hidden[rows, cols] = total.astype(BF)
            return carry

        lax.fori_loop(0, 4, tile, 0)

    for u in range(3):
        z_units[u][1].end()
    lax.fori_loop(0, 4, attended_tile, 0)
    result(0)
    result(1)
    result(2)
    z_units[3][1].end()
    hidden_rows(0)
    z_units[4][1].end()
    hidden_rows(256)
    result(3)
    copies.finish()


def give_back(og_part, grads, wk, wv, wo, wq):
    return pl.pallas_call(
        return_kernel,
        out_shape=[
            jax.ShapeDtypeStruct((512, 1024), BF),
            jax.ShapeDtypeStruct((512, 1024), BF),
            jax.ShapeDtypeStruct((NTOK, 4096), BF),
        ],
        in_specs=[ANY] * 6,
        out_specs=[VM] * 3,
        scratch_shapes=[
            pltpu.VMEM((4096, 512), BF),
            pltpu.VMEM((4096, 512), BF),
            pltpu.VMEM((2048, 1024), BF),
            pltpu.VMEM((1024, 2048), BF),
            pltpu.VMEM((2, 4, 512, 512), BF),
            pltpu.VMEM((2, 512, 512), BF),
            pltpu.VMEM((2, 2, 512, 512), BF),
            pltpu.VMEM((2, 512, 512), BF),
            pltpu.VMEM((2, 4, 512, 512), BF),
            pltpu.VMEM((4, 2, 4, NTOK, 512), BF),
            pltpu.VMEM((4, 2, 4, NTOK, 512), BF),
            pltpu.VMEM((2, 4, NTOK, 512), BF),
            pltpu.VMEM((4, 4, NTOK, 512), BF),
            pltpu.VMEM((2, 4, NTOK, 512), BF),
            pltpu.VMEM((4, NTOK, 4096), BF),
            pltpu.VMEM((2, NTOK, 2048), BF),
            pltpu.VMEM((4, NTOK, 2048), BF),
            pltpu.SemaphoreType.DMA((128,)),
            pltpu.SemaphoreType.DMA((128,)),
            pltpu.SemaphoreType.DMA((32,)),
        ],
        compiler_params=pltpu.CompilerParams(
            collective_id=1, has_side_effects=True, vmem_limit_bytes=60 << 20
        ),
        name="reduce_and_project",
    )(og_part, grads, wk, wv, wo, wq)


def shift_down(rows):
    return jnp.pad(rows[: rows.shape[0] - SPAN + 1], ((SPAN - 1, 0), (0, 0)))


def body(
    hidden, query_weight, key_weight, value_weight, output_weight,
    encoded, location, neighbours, pattern, grad_out,
):
    ids = jnp.pad(neighbours + 256 * pattern, ((0, 0), (0, 126)))
    qg, rows, every_ids, stats = fetch(
        location, hidden, query_weight, encoded.reshape(512, 4096),
        key_weight, value_weight, grad_out, output_weight, ids,
    )
    qg = qg.reshape(2, 32, SPAN, 512)
    og, grads = attend(every_ids, location, qg, rows, stats)
    attended, grad_hidden, grad_encoded = give_back(
        og.reshape(2, 4, 512, 512), grads, key_weight, value_weight, output_weight, query_weight
    )
    return shift_down(attended), shift_down(grad_hidden), grad_encoded.reshape(1, NTOK, 4096)


def solution(mesh):
    return jax.shard_map(
        body,
        mesh=mesh,
        in_specs=(
            P("dp", "head"),
            P("head", None),
            P(None, "head"),
            P(None, "head"),
            P(None, "head"),
            P("dp", None, None),
            P(),
            P("dp", None),
            P("dp", None),
            P("dp", "head"),
        ),
        out_specs=(P("dp", "head"), P("dp", "head"), P(("dp", "head"), None, None)),
        check_vma=False,
    )
```

time: 227 us -> 202 us (0.89); the launches traced: 227 us -> 199 us
  Pallas kernels: 216 us -> 190 us
    pallas_call x2 -> x0, Pallas kernels: 19.6 us -> none  [the longest x1 9.95 us: stats_of(): pl.pallas_call(stats_kernel, out_shape=jax.ShapeDtypeStruct((3, 64, 128),...]
    pallas_call x1, Pallas kernels: 111 us -> 94.8 us  [give_back(): pl.pallas_call(return_kernel, out_shape=[jax.ShapeDtypeStruct((512, 1024)...]
    pallas_call x1, Pallas kernels: 64.1 us -> 75.2 us  [fetch(): pl.pallas_call(fetch_kernel, out_shape=[jax.ShapeDtypeStruct((2, 4, 512,...]
where the time goes in v2:
time: 202 us; the launch traced here: 199 us
  Pallas kernels  190 us (94%)
  local copies, waits for them, and re-layouts  8.57 us (4%)
    pallas_call x1, Pallas kernels, give_back(): pl.pallas_call(return_kernel, out_shape=[jax.ShapeDtypeStruct((512, 1024)...  94.8 us
    pallas_call x1, Pallas kernels, fetch(): pl.pallas_call(fetch_kernel, out_shape=[jax.ShapeDtypeStruct((2, 4, 512,...  75.2 us
    pallas_call x1, Pallas kernels, attend(): pl.pallas_call(attend_kernel, out_shape=[jax.ShapeDtypeStruct((2, 32, SPA...  20 us
    unnamed x13, local copies, waits for them, and re-layouts  4.09 us

profile of v2, /device:TPU:2, one launch (start us, length us, event | category | flops | bytes accessed | tf_op | source)
XLA Modules:
  0.0 199.4 jit_solution(8060033177892758933)
XLA Ops:
  0.6 0.8 copy.14
  1.4 0.8 copy.13
  2.1 0.6 pad.11.ids
  2.7 0.0 copy-start.2
  2.7 75.2 %project_and_gather.1 = (bf16[2,4,512,512]{3,2,1,0:T(8,128)(2,1)}, bf16[8,2,4,128,512]{4,3,2,1,0:T(8,128)(2,1)}, s32[4,8,128]{2,1,0:T(8,128)}, f32[3,64,128]{2,1,0:T(8,128)}) custom-call(s32[128]{0:T(128)} %loc_ref.3, bf16[512,1024]{1,0:T(8,128)(2,1)} %hid.1, bf16[1024,2048]{1,0:T(8,128)(2,1)} %wq.3, bf16[512,4096]{1,0:T(8,128)(2,1)} %bitcast.6, ...), custom_call_target="tpu_custom_call" | custom-call | tf_op jit(solution)/shard_map/project_and_gather/pallas_call | solution.py:423
  78.0 0.0 copy-done.2
  78.0 0.0 copy-start
  78.0 0.9 copy-done
  78.9 0.0 copy-start.1
  78.9 0.7 copy-done.1
  79.6 20.0 %attend_both_ways.1 = (bf16[2,32,64,512]{3,2,1,0:T(8,128)(2,1)}, bf16[8,2,4,128,512]{4,3,2,1,0:T(8,128)(2,1)}) custom-call(s32[4,8,128]{2,1,0:T(8,128)S(1)} %copy-done.1, s32[128]{0:T(128)S(1)} %copy-done.2, bf16[2,32,64,512]{3,2,1,0:T(8,128)(2,1)} %bitcast.5, bf16[8,2,4,128,512]{4,3,2,1,0:T(8,128)(2,1)} %get-tuple-element.14.rows_ref, f32[3,64,128]{2,1,0:T(8,128)S(1)} %copy-done), custom_call_target="tpu_custom_call" | custom-call | tf_op jit(solution)/shard_map/attend_both_ways/pallas_call | solution.py:564
  99.6 94.8 %reduce_and_project.1 = (bf16[512,1024]{1,0:T(8,128)(2,1)}, bf16[512,1024]{1,0:T(8,128)(2,1)}, bf16[128,4096]{1,0:T(8,128)(2,1)}) custom-call(bf16[2,4,512,512]{3,2,1,0:T(8,128)(2,1)} %bitcast.4, bf16[8,2,4,128,512]{4,3,2,1,0:T(8,128)(2,1)} %get-tuple-element.17.grads, bf16[4096,512]{1,0:T(8,128)(2,1)} %wk.3, bf16[4096,512]{1,0:T(8,128)(2,1)} %wv.3, ...), custom_call_target="tpu_custom_call" | custom-call | tf_op jit(solution)/shard_map/reduce_and_project/pallas_call | solution.py:784
  194.5 0.0 copy-start.4
  194.5 0.0 copy-start.3
  194.5 1.4 slice.6
  195.9 1.2 pad.12
  197.1 0.0 copy-done.4
  197.1 0.1 slice.7
  197.2 1.2 pad.13
  198.4 0.0 copy-done.3
  198.4 1.0 copy.16
  (1 shorter events, 0.0 us)
Async XLA Ops:
  2.7 75.2 %copy-start.2 = (s32[128]{0:T(128)S(1)}, s32[128]{0:T(128)}, u32[]{:S(2)}) copy-start(s32[128]{0:T(128)} %loc_ref.3) | copy-start | bytes 1540
  78.0 0.9 copy-start
  78.9 0.7 copy-start.1
  194.5 2.6 %copy-start.4 = (bf16[512,1024]{1,0:T(8,128)(2,1)S(1)}, bf16[512,1024]{1,0:T(8,128)(2,1)}, u32[]{:S(2)}) copy-start(bf16[512,1024]{1,0:T(8,128)(2,1)} %get-tuple-element.19) | copy-start | bytes 3145732
  194.5 3.9 %copy-start.3 = (bf16[128,4096]{1,0:T(8,128)(2,1)S(1)}, bf16[128,4096]{1,0:T(8,128)(2,1)}, u32[]{:S(2)}) copy-start(bf16[128,4096]{1,0:T(8,128)(2,1)} %get-tuple-element.20) | copy-start | bytes 3145732

commit v3 on v2

v3 whole, which is shorter than its diff:
```python
import functools

import jax
import jax.numpy as jnp
from jax import lax
from jax.experimental import pallas as pl
from jax.experimental.pallas import tpu as pltpu
from jax.sharding import PartitionSpec as P

HD = 128
SPAN = 64
NTOK = 128
MESH = pl.DeviceIdType.MESH
BF = jnp.bfloat16
F32 = jnp.float32
NEG = -1e30
SCALE = HD**-0.5
ANY = pl.BlockSpec(memory_space=pl.ANY)
VM = pl.BlockSpec(memory_space=pltpu.VMEM)
SM = pl.BlockSpec(memory_space=pltpu.SMEM)
CHUNKS = 4
TC = NTOK // CHUNKS
SPANS = 8


def dot(a, b, ca, cb):
    return lax.dot_general(a, b, (((ca,), (cb,)), ((), ())), preferred_element_type=F32)


class Ring:
    def __init__(self, me, place):
        self.me = me
        self.p = me + 1 - 2 * (me % 2)
        self.q = 3 - me
        self.far = (me + 2) % 4
        self.dev_p = place(self.p)
        self.dev_q = place(self.q)
        self.dev_far = place(self.far)


def rings():
    dp = lax.axis_index("dp")
    x = lax.axis_index("head")
    z, y, c = dp // 8, (dp // 2) % 4, dp % 2
    ring_z = Ring(z, lambda v: ((v * 4 + y) * 2 + c, x))
    ring_y = Ring(y, lambda v: ((z * 4 + v) * 2 + c, x))
    ring_x = Ring(x, lambda v: (dp, v))
    sister = ((z * 4 + y) * 2 + 1 - c, x)
    return ring_z, ring_y, ring_x, sister, c


def greet(devices):
    barrier = pltpu.get_barrier_semaphore()
    for device in devices:
        pl.semaphore_signal(barrier, inc=1, device_id=device, device_id_type=MESH)
    pl.semaphore_wait(barrier, len(devices))


class Copies:
    def __init__(self, send, recv, local):
        self.send, self.recv, self.local = send, recv, local
        self.remote_count = self.local_count = 0
        self.started = []

    def push(self, src, dst, device):
        index = self.remote_count
        self.remote_count += 1
        copy = pltpu.make_async_remote_copy(
            src_ref=src,
            dst_ref=dst,
            send_sem=self.send.at[index],
            recv_sem=self.recv.at[index],
            device_id=device,
            device_id_type=MESH,
        )
        copy.start()
        self.started.append(copy)
        return copy

    def move(self, src, dst):
        index = self.local_count
        self.local_count += 1
        copy = pltpu.make_async_copy(src, dst, self.local.at[index])
        copy.start()
        return copy

    def finish(self):
        for copy in self.started:
            copy.wait_send()
        self.started = []


class Reduce:
    def __init__(self, copies, ring, part, tmp, got):
        self.copies, self.ring, self.part, self.tmp, self.got = copies, ring, part, tmp, got

    def start(self):
        r, part = self.ring, self.part
        self.to_far = (
            self.copies.push(part(r.far, 0), self.tmp(0), r.dev_p),
            self.copies.push(part(r.far, 1), self.tmp(1), r.dev_q),
        )
        self.near = (
            self.copies.push(part(r.p, 0), self.got(0), r.dev_p),
            self.copies.push(part(r.q, 1), self.got(3), r.dev_q),
        )

    def relay(self, add):
        r, part = self.ring, self.part
        self.to_far[0].wait_recv()
        add(part(r.q, 0), part(r.q, 0), self.tmp(0))
        first = self.copies.push(part(r.q, 0), self.got(2), r.dev_q)
        self.to_far[1].wait_recv()
        add(part(r.p, 1), part(r.p, 1), self.tmp(1))
        second = self.copies.push(part(r.p, 1), self.got(1), r.dev_p)
        self.near = self.near + (first, second)

    def end(self, add, own):
        for copy in self.near:
            copy.wait_recv()
        add(own(0), self.part(self.ring.me, 0), self.got(0), self.got(2))
        add(own(1), self.part(self.ring.me, 1), self.got(1), self.got(3))


class Gather:
    def __init__(self, copies, ring, slot):
        self.copies, self.ring, self.slot = copies, ring, slot

    def start(self, own):
        r = self.ring
        self.to_p = self.copies.push(own, self.slot(r.me), r.dev_p)
        self.to_q = self.copies.push(own, self.slot(r.me), r.dev_q)

    def relay_p(self):
        r = self.ring
        self.to_p.wait_recv()
        self.fwd_q = self.copies.push(self.slot(r.p, 0), self.slot(r.p, 0), r.dev_q)

    def relay_q(self):
        r = self.ring
        self.to_q.wait_recv()
        self.fwd_p = self.copies.push(self.slot(r.q, 1), self.slot(r.q, 1), r.dev_p)

    def relay(self):
        self.relay_p()
        self.relay_q()

    def end(self):
        self.fwd_q.wait_recv()
        self.fwd_p.wait_recv()


def add_up(terms):
    if len(terms) == 2:
        return terms[0] + terms[1]
    return sum(t.astype(F32) for t in terms).astype(BF)


def add_rows(out, *terms):
    if len(out.shape) == 3:
        for index in range(out.shape[0]):
            out[index] = add_up([t[index] for t in terms])
    else:
        out[...] = add_up([t[...] for t in terms])


def kernel(
    loc_ref, hid, wq, enc, wk, wv, gout, wo, ids,
    attended, grad_hidden, grad_encoded, ids_out,
    v_hid, v_gout, shifted, wide, v_wk, v_wv, v_enc, part, tmp, got, qg, rows,
    ids_ref, stored_ref, table_ref, stats, held,
    c_got, y_tmp, y_got, mine, x_tmp, x_got, send, recv, local,
):
    ring_z, ring_y, ring_x, sister, c = rings()
    copies = Copies(send, recv, local)
    plane = lax.axis_index("dp") // 8

    def load_wide(which):
        if which == 0:
            return [copies.move(wq.at[:, :, pl.ds(g * 512, 512)], wide.at[pl.ds(g * 8, 8)]) for g in range(4)]
        return [copies.move(wo.at[:, :, pl.ds(j * 512, 512)], wide.at[pl.ds(32 + j * 16, 16)]) for j in range(2)]

    load_hid = copies.move(hid, v_hid)
    load_wq = load_wide(0)
    load_enc = [
        copies.move(enc.at[:, :, pl.ds(j * 512, 512)], v_enc.at[j // 4, j % 4]) for j in range(8)
    ]
    load_wk = copies.move(wk, v_wk)
    load_wv = copies.move(wv, v_wv)
    load_gout = copies.move(gout, v_gout)
    load_wo = load_wide(1)
    greet(
        [ring_x.dev_p, ring_x.dev_q, ring_y.dev_p, ring_y.dev_q, ring_z.dev_p, ring_z.dev_q, ring_z.dev_far, sister]
    )
    id_copies = [
        copies.push(ids, ids_out.at[ring_z.me], d) for d in (ring_z.dev_p, ring_z.dev_q, ring_z.dev_far)
    ]
    own_ids = copies.move(ids, ids_out.at[ring_z.me])


    def unit_of(w, u):
        reduce = Reduce(
            copies,
            ring_x,
            lambda i, half: part.at[w, i, 2 * u + half],
            lambda half: tmp.at[w, 2 * u + half],
            lambda k: got.at[w, k // 2, 2 * u + k % 2],
        )

        def slot(i, half=None):
            return qg.at[w, i, pl.ds(2 * u, 2)] if half is None else qg.at[w, i, 2 * u + half]

        return reduce, Gather(copies, ring_z, slot)

    units = [unit_of(n // 4, n % 4) for n in range(8)]

    def shift_tile(ref, t):
        first = min(t, 2) * 128
        row = lax.broadcasted_iota(jnp.int32, (128, 256), 0) + (t * 128 + SPAN - 1 - first)
        col = lax.broadcasted_iota(jnp.int32, (128, 256), 1)
        move = (row == col).astype(BF)
        shifted[pl.ds(t * 128, 128), :] = dot(move, ref[pl.ds(first, 256), :], 1, 0).astype(BF)

    def query_rows(first, size):
        def tile(g, carry):
            here = pl.ds(first, size)
            weight = wide[pl.ds(pl.multiple_of(g * 8, 8), 8)].reshape(1024, 512)
            product = dot(shifted[here, :], weight, 1, 0).astype(BF)
            part[0, g, pl.ds(first // SPAN, size // SPAN)] = product.reshape(size // SPAN, SPAN, 512)
            return carry

        lax.fori_loop(0, 4, tile, 0)

    def output_block(g, j):
        return wide[pl.ds(32 + j * 16 + g * 4, 4)].reshape(512, 512)

    def begin(n):
        units[n][0].start()

    def relay(n):
        units[n][0].relay(add_rows)

    def reduced(n):
        reduce, gather = units[n]
        reduce.end(add_rows, lambda half: gather.slot(ring_z.me, half))
        gather.start(gather.slot(ring_z.me))

    def spread(n):
        units[n][1].relay()


    streams = []

    def project(s, weight):
        own = rows.at[ring_y.me * 2 + c, s]

        def tile(j, carry):
            cols = pl.ds(pl.multiple_of(j * 256, 256), 256)
            total = dot(v_enc[0, 0].reshape(512, 512), weight[0:512, cols], 1, 0)
            for k in range(1, 8):
                block = v_enc[k // 4, k % 4].reshape(512, 512)
                total = total + dot(block, weight[k * 512 : (k + 1) * 512, cols], 1, 0)
            own[:, :, cols] = total.astype(BF).reshape(4, NTOK, 256)
            return carry

        lax.fori_loop(0, 2, tile, 0)

        def slot(i, half=None):
            block = rows.at[i * 2 + c, s]
            return block if half is None else block.at[pl.ds((half + s) % 2 * 2, 2)]

        gather = Gather(copies, ring_y, slot)
        gather.start(own)
        streams.append((gather, [copies.push(own, own, sister)]))

    def forward(s):
        gather, to_sister = streams[s]
        gather.relay_p()
        to_sister.append(copies.push(gather.slot(ring_y.p), gather.slot(ring_y.p), sister))
        gather.relay_q()
        to_sister.append(copies.push(gather.slot(ring_y.q), gather.slot(ring_y.q), sister))

    def forwarded(s):
        gather, to_sister = streams[s]
        gather.fwd_q.wait_recv()
        to_sister.append(copies.push(gather.slot(ring_y.far, 0), gather.slot(ring_y.far, 0), sister))
        gather.fwd_p.wait_recv()
        to_sister.append(copies.push(gather.slot(ring_y.far, 1), gather.slot(ring_y.far, 1), sister))

    load_hid.wait()
    shift_tile(v_hid, 0)
    for load in load_wq:
        load.wait()
    query_rows(0, 128)
    begin(0)
    for t in range(1, 4):
        shift_tile(v_hid, t)
    query_rows(128, 384)
    begin(1)
    relay(0)
    begin(2)
    for load in load_enc:
        load.wait()
    load_wk.wait()
    project(0, v_wk)
    relay(1)
    begin(3)
    reduced(0)
    load_wv.wait()
    project(1, v_wv)
    relay(2)
    reduced(1)
    load_gout.wait()
    for t in range(4):
        shift_tile(v_gout, t)
    for load in load_wo:
        load.wait()

    def grad_tile(g, carry):
        total = dot(shifted[:, 0:512], output_block(g, 0), 1, 1)
        total = total + dot(shifted[:, 512:1024], output_block(g, 1), 1, 1)
        part[1, g] = total.astype(BF).reshape(SPANS, SPAN, 512)
        return carry

    lax.fori_loop(0, 4, grad_tile, 0)
    begin(4)
    relay(3)
    begin(5)
    reduced(2)
    spread(0)
    relay(4)
    begin(6)
    reduced(3)
    spread(1)
    forward(0)
    relay(5)
    begin(7)
    reduced(4)
    spread(2)
    relay(6)
    reduced(5)
    spread(3)
    forward(1)
    for copy in id_copies:
        copy.wait_recv()
    own_ids.wait()
    copies.move(ids_out, ids_ref).wait()


    def store_row(n, carry):
        entry = ids_ref[n // 16, n // 2 % 8, n % 2]
        live = (entry >= 256).astype(jnp.int32)
        stored_ref[n] = (loc_ref[entry % 256] + 1) * live - 1
        return carry

    lax.fori_loop(0, 64, store_row, 0)

    def list_slots(n, carry):
        block = n // 4 + plane * 8
        sequence = n % 4
        count = first = second = row = 0
        for e in range(16):
            stored = stored_ref[sequence * 16 + e]
            match = jnp.logical_and(stored >= 0, stored // 4 == block).astype(jnp.int32)
            one = match * (count == 0).astype(jnp.int32) if e else match
            two = match - one
            first, second = first + one * e, second + two * e
            row = row + one * (stored % 4)
            count = count + match
        table_ref[0, n] = first
        table_ref[1, n] = second
        table_ref[2, n] = count
        table_ref[3, n] = row
        return carry

    lax.fori_loop(0, 32, list_slots, 0)
    relay(7)
    reduced(6)
    spread(4)
    reduced(7)
    spread(5)
    forwarded(0)
    spread(6)
    forwarded(1)
    spread(7)
    for n in range(4):
        units[n][1].end()
    for _, to_sister in streams:
        for copy in to_sister:
            copy.wait_recv()

    def memory_of(n, cols):
        stored = stored_ref[n]
        live = jnp.logical_and(stored >= 0, stored // 32 == plane).astype(F32)
        row = (stored + 32) % 32
        return rows[row // 4, 0, row % 4, :, cols], rows[row // 4, 1, row % 4, :, cols], live

    def stats_of_spans(first):
        def span(j, carry):
            sequence, place = j // 2, first + j % 2
            i = sequence * 8 + place
            for pair in range(2):
                cols = pl.ds(pair * 256, 256)
                query = two_heads(qg[0, sequence, place, :, cols])
                grad = two_heads(qg[1, sequence, place, :, cols])
                made = []
                for k in range(2):
                    key, value, live = memory_of(i * 2 + k, cols)
                    score = dot(key, query, 1, 1) * SCALE
                    gw = dot(value, grad, 1, 1)
                    top = jnp.max(score, axis=0, keepdims=True)
                    e = jnp.exp(score - top)
                    total = jnp.sum(e, axis=0, keepdims=True) * live
                    inner = jnp.sum(e * gw, axis=0, keepdims=True) * live
                    made.append((top * live + NEG * (1.0 - live), total, inner))
                (top0, sum0, dot0), (top1, sum1, dot1) = made
                top = jnp.maximum(top0, top1)
                f0, f1 = jnp.exp(top0 - top), jnp.exp(top1 - top)
                line = pl.ds(i * 2 + pair, 1)
                stats[0, line, :] = top
                stats[1, line, :] = sum0 * f0 + sum1 * f1
                stats[2, line, :] = dot0 * f0 + dot1 * f1
            return carry

        lax.fori_loop(0, 8, span, 0)

    for u in range(4):
        units[4 + u][1].end()
        stats_of_spans(2 * u)

    def stats_slot(i, half=None):
        return held.at[i] if half is None else held.at[i, :, pl.ds(half * 32, 32)]

    exchange = Gather(copies, ring_z, stats_slot)
    exchange.start(stats)
    held[ring_z.me] = stats[...]
    exchange.relay()
    exchange.end()
    copies.finish()
    tops = [held[k, 0] for k in range(4)]
    top = jnp.maximum(jnp.maximum(tops[0], tops[1]), jnp.maximum(tops[2], tops[3]))
    fades = [jnp.exp(t - top) for t in tops]
    total = sum(fades[k] * held[k, 1] for k in range(4))
    inner = sum(fades[k] * held[k, 2] for k in range(4))
    stats[0] = top
    stats[1] = 1.0 / total
    stats[2] = inner / total


    def attend_spans(first):
        def span(j, carry):
            sequence, place = j // 2, first + j % 2
            i = sequence * 8 + place
            for pair in range(2):
                cols = pl.ds(pair * 256, 256)
                query = two_heads(qg[0, sequence, place, :, cols])
                grad = two_heads(qg[1, sequence, place, :, cols])
                line = pl.ds(i * 2 + pair, 1)
                keys, values, ws, dss = [], [], [], []
                for k in range(2):
                    key, value, live = memory_of(i * 2 + k, cols)
                    score = dot(key, query, 1, 1) * SCALE
                    gw = dot(value, grad, 1, 1)
                    share = stats[1, line, :] * live
                    w = jnp.exp(jnp.minimum(score - stats[0, line, :], 0.0)) * share
                    ds = (w * (gw - stats[2, line, :]) * SCALE).astype(BF)
                    w = w.astype(BF)
                    wide[i * 2 + k, :, pl.ds(pair * 128, 128)] = w
                    wide[i * 2 + k, :, pl.ds(256 + pair * 128, 128)] = ds
                    keys.append(key)
                    values.append(value)
                    ws.append(w)
                    dss.append(ds)
                for which, probs, memory in ((0, ws, values), (1, dss, keys)):
                    out = dot(jnp.concatenate(probs, axis=0), jnp.concatenate(memory, axis=0), 0, 0)
                    for h in range(2):
                        part[which, sequence, place, :, pl.ds(pair * 256 + h * HD, HD)] = out[
                            h * SPAN : (h + 1) * SPAN, h * HD : (h + 1) * HD
                        ].astype(BF)
            return carry

        lax.fori_loop(0, 8, span, 0)

    def row_grads(block):
        for pair in range(2):
            cols = pl.ds(pair * 256, 256)
            for kv in range(2):
                made = []
                for sequence in range(4):
                    n = block * 4 + sequence
                    first, second = table_ref[0, n], table_ref[1, n]
                    both = (table_ref[2, n] >= 2).astype(F32)
                    place = pl.ds((256 if kv == 0 else 0) + pair * 128, 128)
                    probs = jnp.concatenate(
                        [
                            wide[sequence * 16 + first, :, place],
                            wide[sequence * 16 + second, :, place] * both.astype(BF),
                        ],
                        axis=1,
                    )
                    other = jnp.concatenate(
                        [
                            two_heads(qg[kv, sequence, first // 2, :, cols]),
                            two_heads(qg[kv, sequence, second // 2, :, cols]),
                        ],
                        axis=0,
                    )
                    made.append(dot(probs, other, 1, 0).astype(BF))
                for r in range(4):
                    total = None
                    for sequence in range(4):
                        n = block * 4 + sequence
                        pick = jnp.logical_and(table_ref[2, n] >= 1, table_ref[3, n] == r)
                        term = made[sequence] * pick.astype(F32).astype(BF)
                        total = term if total is None else total + term
                    rows[block, kv, r, :, cols] = total


    def z_unit(w, u):
        reduce = Reduce(
            copies,
            ring_z,
            lambda i, half: part.at[w, i, 2 * u + half],
            lambda half: tmp.at[w, 2 * u + half],
            lambda k: got.at[w, k // 2, 2 * u + k % 2],
        )

        def slot(i, half=None):
            return v_enc.at[w, i, pl.ds(2 * u, 2)] if half is None else v_enc.at[w, i, 2 * u + half]

        return reduce, Gather(copies, ring_x, slot)

    outs = [[z_unit(w, u) for u in range(4)] for w in range(2)]

    def zb(w, u):
        outs[w][u][0].start()

    def zr(w, u):
        outs[w][u][0].relay(add_rows)

    def zd(w, u):
        reduce, gather = outs[w][u]
        reduce.end(add_rows, lambda half: gather.slot(ring_x.me, half))
        gather.start(gather.slot(ring_x.me))

    def zs(w, u):
        outs[w][u][1].relay()


    order = (ring_y.far, ring_y.p, ring_y.q, ring_y.me)

    def y_unit(t):
        here = pl.ds(t * TC, TC)
        by_row = Reduce(
            copies,
            ring_y,
            lambda i, half: rows.at[i * 2 + c, half, :, here],
            lambda half: y_tmp.at[half, t],
            lambda k: y_got.at[k, t],
        )
        by_group = Reduce(
            copies,
            ring_x,
            lambda i, half: qg.at[half, :, i * 2 + t // 2, pl.ds(t % 2 * TC, TC)],
            lambda half: x_tmp.at[half, t],
            lambda k: x_got.at[k, t],
        )
        return by_row, by_group

    chunks = [y_unit(t) for t in range(CHUNKS)]
    swaps = []

    def sister_rows(k):
        block = order[k] * 2 + 1 - c
        row_grads(block)
        swaps.append(copies.push(rows.at[block], c_got.at[order[k]], sister))

    def own_rows(k):
        row_grads(order[k] * 2 + c)

    def y_start(t):
        here = pl.ds(t * TC, TC)
        for k, i in enumerate(order):
            if t == 0:
                swaps[k].wait_recv()
            for half in range(2):
                block = rows.at[i * 2 + c, half, :, here]
                add_rows(block, block, c_got.at[i, half, :, here])
        chunks[t][0].start()

    def y_relay(t):
        chunks[t][0].relay(add_rows)

    def y_done(t):
        chunks[t][0].end(add_rows, lambda half: mine.at[half])

        def tile(j, carry):
            cols = pl.ds(pl.multiple_of(j * 512, 512), 512)
            keys = mine[0].reshape(4 * TC, 512)
            values = mine[1].reshape(4 * TC, 512)
            product = dot(keys, v_wk[cols, :], 1, 1) + dot(values, v_wv[cols, :], 1, 1)
            product = product.astype(BF)
            for r in range(4):
                qg[j // 4, j % 4, r * 2 + t // 2, pl.ds(t % 2 * TC, TC), :] = product[r * TC : (r + 1) * TC]
            return carry

        lax.fori_loop(0, 8, tile, 0)
        chunks[t][1].start()

    def x_relay(t):
        chunks[t][1].relay(add_rows)

    def result(t):
        chunks[t][1].end(
            add_rows, lambda half: grad_encoded.at[pl.ds(half * 4, 4), pl.ds(t * TC, TC)]
        )

    attend_spans(0)
    zb(0, 0)
    attend_spans(2)
    zr(0, 0)
    zb(1, 0)
    zb(0, 1)
    attend_spans(4)
    zd(0, 0)
    zr(1, 0)
    zr(0, 1)
    zb(1, 1)
    attend_spans(6)
    zd(1, 0)
    zd(0, 1)
    zb(0, 2)
    sister_rows(0)
    zr(1, 1)
    zb(1, 2)
    zs(0, 0)
    sister_rows(1)
    zd(1, 1)
    zs(1, 0)
    sister_rows(2)
    zr(0, 2)
    zb(0, 3)
    zs(0, 1)
    sister_rows(3)
    zd(0, 2)
    zr(1, 2)
    zb(1, 3)
    own_rows(0)
    own_rows(1)
    zd(1, 2)
    zs(1, 1)
    own_rows(2)
    own_rows(3)
    again = load_wide(0) + load_wide(1)
    zr(0, 3)
    y_start(0)
    y_start(1)
    zd(0, 3)
    zs(0, 2)
    zr(1, 3)
    y_relay(0)
    y_start(2)
    zd(1, 3)
    zs(1, 2)
    y_done(0)
    y_relay(1)
    y_start(3)
    zs(0, 3)
    y_done(1)
    x_relay(0)
    y_relay(2)
    zs(1, 3)
    y_done(2)
    x_relay(1)
    y_relay(3)
    x_relay(2)
    y_done(3)
    for load in again:
        load.wait()
    for u in range(4):
        outs[0][u][1].end()

    def everyone(w, g, first, size):
        return v_enc[w, g, pl.ds(first // SPAN, size // SPAN)].reshape(size, 512)

    def attended_tile(j, carry):
        cols = pl.ds(pl.multiple_of(j % 2 * 256, 256), 256)
        total = None
        for g in range(4):
            weight = wide[pl.ds(32 + j // 2 * 16 + g * 4, 4), :, cols].reshape(512, 256)
            term = dot(everyone(0, g, 0, 512), weight, 1, 0)
            total = term if total is None else total + term
        attended[:, pl.ds(pl.multiple_of(j * 256, 256), 256)] = total.astype(BF)
        return carry

    def hidden_rows(first):
        def tile(j, carry):
            total = None
            for g in range(4):
                weight = wide[pl.ds(g * 8 + j * 2, 2)].reshape(256, 512)
                term = dot(everyone(1, g, first, 256), weight, 1, 1)
                total = term if total is None else total + term
            grad_hidden[pl.ds(first, 256), pl.ds(pl.multiple_of(j * 256, 256), 256)] = total.astype(BF)
            return carry

        lax.fori_loop(0, 4, tile, 0)

    lax.fori_loop(0, 4, attended_tile, 0)
    x_relay(3)
    result(0)
    result(1)
    result(2)
    for u in range(2):
        outs[1][u][1].end()
    hidden_rows(0)
    for u in range(2, 4):
        outs[1][u][1].end()
    hidden_rows(256)
    result(3)
    copies.finish()


def cross_attention(loc, hid, wq, enc, wk, wv, gout, wo, ids):
    return pl.pallas_call(
        kernel,
        out_shape=[
            jax.ShapeDtypeStruct((512, 1024), BF),
            jax.ShapeDtypeStruct((512, 1024), BF),
            jax.ShapeDtypeStruct((8, NTOK, 512), BF),
            jax.ShapeDtypeStruct((4, 8, 128), jnp.int32),
        ],
        in_specs=[SM] + [ANY] * 8,
        out_specs=[VM, VM, VM, ANY],
        scratch_shapes=[
            pltpu.VMEM((512, 1024), BF),
            pltpu.VMEM((512, 1024), BF),
            pltpu.VMEM((512, 1024), BF),
            pltpu.VMEM((64, 128, 512), BF),
            pltpu.VMEM((4096, 512), BF),
            pltpu.VMEM((4096, 512), BF),
            pltpu.VMEM((2, 4, SPANS, SPAN, 512), BF),
            pltpu.VMEM((2, 4, SPANS, SPAN, 512), BF),
            pltpu.VMEM((2, SPANS, SPAN, 512), BF),
            pltpu.VMEM((2, 2, SPANS, SPAN, 512), BF),
            pltpu.VMEM((2, 4, SPANS, SPAN, 512), BF),
            pltpu.VMEM((8, 2, 4, NTOK, 512), BF),
            pltpu.SMEM((4, 8, 128), jnp.int32),
            pltpu.SMEM((64,), jnp.int32),
            pltpu.SMEM((4, 32), jnp.int32),
            pltpu.VMEM((3, 64, 128), F32),
            pltpu.VMEM((4, 3, 64, 128), F32),
            pltpu.VMEM((4, 2, 4, NTOK, 512), BF),
            pltpu.VMEM((2, CHUNKS, 4, TC, 512), BF),
            pltpu.VMEM((4, CHUNKS, 4, TC, 512), BF),
            pltpu.VMEM((2, 4, TC, 512), BF),
            pltpu.VMEM((2, CHUNKS, 4, TC, 512), BF),
            pltpu.VMEM((4, CHUNKS, 4, TC, 512), BF),
            pltpu.SemaphoreType.DMA((256,)),
            pltpu.SemaphoreType.DMA((256,)),
            pltpu.SemaphoreType.DMA((40,)),
        ],
        compiler_params=pltpu.CompilerParams(
            collective_id=0, has_side_effects=True, vmem_limit_bytes=62 << 20
        ),
        name="cross_attention",
    )(loc, hid, wq, enc, wk, wv, gout, wo, ids)


def two_heads(block):
    zero = jnp.zeros((SPAN, HD), BF)
    return jnp.concatenate(
        [
            jnp.concatenate([block[:, :HD], zero], axis=1),
            jnp.concatenate([zero, block[:, HD:]], axis=1),
        ],
        axis=0,
    )


def shift_down(rows):
    return jnp.pad(rows[: rows.shape[0] - SPAN + 1], ((SPAN - 1, 0), (0, 0)))


def body(
    hidden, query_weight, key_weight, value_weight, output_weight,
    encoded, location, neighbours, pattern, grad_out,
):
    ids = jnp.pad(neighbours + 256 * pattern, ((0, 0), (0, 126)))
    attended, grad_hidden, grad_encoded, _ = cross_attention(
        location, hidden, query_weight.reshape(8, 128, 2048), encoded.reshape(8, 64, 4096),
        key_weight, value_weight, grad_out, output_weight.reshape(16, 128, 1024), ids,
    )
    grad_encoded = jnp.transpose(grad_encoded, (1, 0, 2)).reshape(1, NTOK, 4096)
    return shift_down(attended), shift_down(grad_hidden), grad_encoded


def solution(mesh):
    return jax.shard_map(
        body,
        mesh=mesh,
        in_specs=(
            P("dp", "head"),
            P("head", None),
            P(None, "head"),
            P(None, "head"),
            P(None, "head"),
            P("dp", None, None),
            P(),
            P("dp", None),
            P("dp", None),
            P("dp", "head"),
        ),
        out_specs=(P("dp", "head"), P("dp", "head"), P(("dp", "head"), None, None)),
        check_vma=False,
    )
```

time: 202 us -> 193 us (0.955)
  Pallas kernels: 190 us -> 183 us
    pallas_call x3 -> x1, Pallas kernels: 190 us -> 183 us  [cross_attention(): pl.pallas_call(kernel, out_shape=[jax.ShapeDtypeStruct((512, 1024), BF),...]
    unnamed x13 -> x7, local copies, waits for them, and re-layouts: 4.09 us -> 2.83 us
where the time goes in v3:
time: 193 us; the launch traced here: 192 us
  Pallas kernels  183 us (95%)
  local copies, waits for them, and re-layouts  7.96 us (4%)
    pallas_call x1, Pallas kernels, cross_attention(): pl.pallas_call(kernel, out_shape=[jax.ShapeDtypeStruct((512, 1024), BF),...  183 us

profile of v3, /device:TPU:2, one launch (start us, length us, event | category | flops | bytes accessed | tf_op | source)
XLA Modules:
  0.0 192.0 jit_solution(14971653753962045365)
XLA Ops:
  0.6 0.8 copy.16
  1.4 0.8 copy.15
  2.1 0.6 pad.11.ids
  2.7 183.3 %cross_attention.1 = (bf16[512,1024]{1,0:T(8,128)(2,1)}, bf16[512,1024]{1,0:T(8,128)(2,1)}, bf16[8,128,512]{2,1,0:T(8,128)(2,1)}, s32[4,8,128]{2,1,0:T(8,128)}) custom-call(s32[128]{0:T(128)} %loc_ref.1, bf16[512,1024]{1,0:T(8,128)(2,1)} %hid.1, bf16[8,128,2048]{2,1,0:T(8,128)(2,1)} %bitcast.6, bf16[8,64,4096]{2,1,0:T(8,128)(2,1)} %bitcast.7, ...), custom_call_target="tpu_custom_call" | custom-call | tf_op jit(solution)/shard_map/cross_attention/pallas_call | solution.py:724
  186.1 0.0 copy-start.1
  186.1 0.0 copy-start
  186.1 1.4 slice.6
  187.5 1.2 pad.12
  188.7 0.0 copy-done.1
  188.7 0.1 slice.7
  188.8 1.2 pad.13
  190.0 0.0 copy-done
  190.0 0.7 copy.17
  190.7 1.3 copy.18
  (1 shorter events, 0.0 us)
Async XLA Ops:
  186.1 2.6 %copy-start.1 = (bf16[512,1024]{1,0:T(8,128)(2,1)S(1)}, bf16[512,1024]{1,0:T(8,128)(2,1)}, u32[]{:S(2)}) copy-start(bf16[512,1024]{1,0:T(8,128)(2,1)} %get-tuple-element.7) | copy-start | bytes 3145732
  186.1 3.9 %copy-start = (bf16[8,128,512]{2,1,0:T(8,128)(2,1)S(1)}, bf16[8,128,512]{2,1,0:T(8,128)(2,1)}, u32[]{:S(2)}) copy-start(bf16[8,128,512]{2,1,0:T(8,128)(2,1)} %get-tuple-element.8) | copy-start | bytes 3145732

commit v4 on v3

--- a/solution.py
+++ b/solution.py
@@ -18,7 +18,7 @@
 ANY = pl.BlockSpec(memory_space=pl.ANY)
 VM = pl.BlockSpec(memory_space=pltpu.VMEM)
 SM = pl.BlockSpec(memory_space=pltpu.SMEM)
-CHUNKS = 4
+CHUNKS = 2
 TC = NTOK // CHUNKS
 SPANS = 8
 
@@ -60,7 +60,7 @@
     def __init__(self, send, recv, local):
         self.send, self.recv, self.local = send, recv, local
         self.remote_count = self.local_count = 0
-        self.started = []
+        self.started = {}
 
     def push(self, src, dst, device):
         index = self.remote_count
@@ -74,7 +74,7 @@
             device_id_type=MESH,
         )
         copy.start()
-        self.started.append(copy)
+        self.started[id(copy)] = copy
         return copy
 
     def move(self, src, dst):
@@ -84,10 +84,13 @@
         copy.start()
         return copy
 
+    def settle(self, copy):
+        if self.started.pop(id(copy), None) is not None:
+            copy.wait_send()
+
     def finish(self):
-        for copy in self.started:
-            copy.wait_send()
-        self.started = []
+        for copy in list(self.started.values()):
+            self.settle(copy)
 
 
 class Reduce:
@@ -104,6 +107,10 @@
             self.copies.push(part(r.p, 0), self.got(0), r.dev_p),
             self.copies.push(part(r.q, 1), self.got(3), r.dev_q),
         )
+
+    def sent(self):
+        for copy in self.to_far + self.near:
+            self.copies.settle(copy)
 
     def relay(self, add):
         r, part = self.ring, self.part
@@ -293,23 +300,21 @@
         load.wait()
     query_rows(0, 128)
     begin(0)
+    for load in load_enc:
+        load.wait()
+    load_wk.wait()
+    project(0, v_wk)
     for t in range(1, 4):
         shift_tile(v_hid, t)
     query_rows(128, 384)
     begin(1)
     relay(0)
     begin(2)
-    for load in load_enc:
-        load.wait()
-    load_wk.wait()
-    project(0, v_wk)
+    load_wv.wait()
+    project(1, v_wv)
     relay(1)
     begin(3)
     reduced(0)
-    load_wv.wait()
-    project(1, v_wv)
-    relay(2)
-    reduced(1)
     load_gout.wait()
     for t in range(4):
         shift_tile(v_gout, t)
@@ -323,22 +328,22 @@
         return carry
 
     lax.fori_loop(0, 4, grad_tile, 0)
+    relay(2)
     begin(4)
+    reduced(1)
+    spread(0)
     relay(3)
     begin(5)
     reduced(2)
-    spread(0)
+    spread(1)
+    forward(0)
     relay(4)
     begin(6)
     reduced(3)
-    spread(1)
-    forward(0)
+    spread(2)
     relay(5)
     begin(7)
     reduced(4)
-    spread(2)
-    relay(6)
-    reduced(5)
     spread(3)
     forward(1)
     for copy in id_copies:
@@ -374,20 +379,20 @@
         return carry
 
     lax.fori_loop(0, 32, list_slots, 0)
+    relay(6)
+    reduced(5)
+    spread(4)
     relay(7)
     reduced(6)
-    spread(4)
-    reduced(7)
     spread(5)
     forwarded(0)
-    spread(6)
+    reduced(7)
     forwarded(1)
-    spread(7)
-    for n in range(4):
-        units[n][1].end()
-    for _, to_sister in streams:
-        for copy in to_sister:
-            copy.wait_recv()
+
+    def rows_complete():
+        for _, to_sister in streams:
+            for copy in to_sister:
+                copy.wait_recv()
 
     def memory_of(n, cols):
         stored = stored_ref[n]
@@ -403,48 +408,64 @@
                 cols = pl.ds(pair * 256, 256)
                 query = two_heads(qg[0, sequence, place, :, cols])
                 grad = two_heads(qg[1, sequence, place, :, cols])
+                top = jnp.full((1, 128), NEG, F32)
                 made = []
                 for k in range(2):
                     key, value, live = memory_of(i * 2 + k, cols)
                     score = dot(key, query, 1, 1) * SCALE
                     gw = dot(value, grad, 1, 1)
-                    top = jnp.max(score, axis=0, keepdims=True)
-                    e = jnp.exp(score - top)
-                    total = jnp.sum(e, axis=0, keepdims=True) * live
-                    inner = jnp.sum(e * gw, axis=0, keepdims=True) * live
-                    made.append((top * live + NEG * (1.0 - live), total, inner))
-                (top0, sum0, dot0), (top1, sum1, dot1) = made
-                top = jnp.maximum(top0, top1)
-                f0, f1 = jnp.exp(top0 - top), jnp.exp(top1 - top)
-                line = pl.ds(i * 2 + pair, 1)
-                stats[0, line, :] = top
-                stats[1, line, :] = sum0 * f0 + sum1 * f1
-                stats[2, line, :] = dot0 * f0 + dot1 * f1
+                    high = jnp.max(score, axis=0, keepdims=True)
+                    top = jnp.maximum(top, high * live + NEG * (1.0 - live))
+                    made.append((score, gw, live))
+                total, inner = 0.0, 0.0
+                for k in range(2):
+                    score, gw, live = made[k]
+                    e = jnp.exp(jnp.minimum(score - top, 0.0)) * live
+                    total = total + jnp.sum(e, axis=0, keepdims=True)
+                    inner = inner + jnp.sum(e * gw, axis=0, keepdims=True)
+                    wide[i * 2 + k, :, pl.ds(pair * 128, 128)] = e.astype(BF)
+                    wide[i * 2 + k, :, pl.ds(256 + pair * 128, 128)] = gw.astype(BF)
+                line = pl.ds(first * 8 + j * 2 + pair, 1)
+                held[ring_z.me, 0, line, :] = top
+                held[ring_z.me, 1, line, :] = total
+                held[ring_z.me, 2, line, :] = inner
             return carry
 
         lax.fori_loop(0, 8, span, 0)
 
-    for u in range(4):
+    def exchange_of(u):
+        def slot(i, half=None):
+            return held.at[i, :, pl.ds(u * 16, 16) if half is None else pl.ds(u * 16 + half * 8, 8)]
+
+        return Gather(copies, ring_z, slot)
+
+    exchanges = [exchange_of(u) for u in range(4)]
+
+    def unit_stats(u):
+        units[u][1].end()
         units[4 + u][1].end()
         stats_of_spans(2 * u)
 
-    def stats_slot(i, half=None):
-        return held.at[i] if half is None else held.at[i, :, pl.ds(half * 32, 32)]
-
-    exchange = Gather(copies, ring_z, stats_slot)
-    exchange.start(stats)
-    held[ring_z.me] = stats[...]
-    exchange.relay()
-    exchange.end()
-    copies.finish()
-    tops = [held[k, 0] for k in range(4)]
-    top = jnp.maximum(jnp.maximum(tops[0], tops[1]), jnp.maximum(tops[2], tops[3]))
-    fades = [jnp.exp(t - top) for t in tops]
-    total = sum(fades[k] * held[k, 1] for k in range(4))
-    inner = sum(fades[k] * held[k, 2] for k in range(4))
-    stats[0] = top
-    stats[1] = 1.0 / total
-    stats[2] = inner / total
+    def exchange_start(u):
+        exchanges[u].start(exchanges[u].slot(ring_z.me))
+
+    def exchange_relay(u):
+        exchanges[u].relay()
+
+    def exchange_end(u):
+        exchanges[u].end()
+        here = pl.ds(u * 16, 16)
+        tops = [held[k, 0, here] for k in range(4)]
+        top = jnp.maximum(jnp.maximum(tops[0], tops[1]), jnp.maximum(tops[2], tops[3]))
+        fades = [jnp.exp(t - top) for t in tops]
+        total = sum(fades[k] * held[k, 1, here] for k in range(4))
+        inner = sum(fades[k] * held[k, 2, here] for k in range(4))
+        stats[0, here] = jnp.exp(held[ring_z.me, 0, here] - top) / total
+        stats[1, here] = inner / total
+
+    def first_sends_done(u):
+        units[u][0].sent()
+        units[4 + u][0].sent()
 
 
     def attend_spans(first):
@@ -453,20 +474,19 @@
             i = sequence * 8 + place
             for pair in range(2):
                 cols = pl.ds(pair * 256, 256)
-                query = two_heads(qg[0, sequence, place, :, cols])
-                grad = two_heads(qg[1, sequence, place, :, cols])
-                line = pl.ds(i * 2 + pair, 1)
+                line = pl.ds(first * 8 + j * 2 + pair, 1)
+                share = stats[0, line, :]
+                center = stats[1, line, :]
                 keys, values, ws, dss = [], [], [], []
                 for k in range(2):
-                    key, value, live = memory_of(i * 2 + k, cols)
-                    score = dot(key, query, 1, 1) * SCALE
-                    gw = dot(value, grad, 1, 1)
-                    share = stats[1, line, :] * live
-                    w = jnp.exp(jnp.minimum(score - stats[0, line, :], 0.0)) * share
-                    ds = (w * (gw - stats[2, line, :]) * SCALE).astype(BF)
+                    key, value, _ = memory_of(i * 2 + k, cols)
+                    lane_w, lane_s = pl.ds(pair * 128, 128), pl.ds(256 + pair * 128, 128)
+                    w = wide[i * 2 + k, :, lane_w].astype(F32) * share
+                    gw = wide[i * 2 + k, :, lane_s].astype(F32)
+                    ds = (w * (gw - center) * SCALE).astype(BF)
                     w = w.astype(BF)
-                    wide[i * 2 + k, :, pl.ds(pair * 128, 128)] = w
-                    wide[i * 2 + k, :, pl.ds(256 + pair * 128, 128)] = ds
+                    wide[i * 2 + k, :, lane_w] = w
+                    wide[i * 2 + k, :, lane_s] = ds
                     keys.append(key)
                     values.append(value)
                     ws.append(w)
@@ -561,7 +581,7 @@
         by_group = Reduce(
             copies,
             ring_x,
-            lambda i, half: qg.at[half, :, i * 2 + t // 2, pl.ds(t % 2 * TC, TC)],
+            lambda i, half: qg.at[half, :, i * 2 + t * TC // SPAN, pl.ds(t * TC % SPAN, TC)],
             lambda half: x_tmp.at[half, t],
             lambda k: x_got.at[k, t],
         )
@@ -601,7 +621,7 @@
             product = dot(keys, v_wk[cols, :], 1, 1) + dot(values, v_wv[cols, :], 1, 1)
             product = product.astype(BF)
             for r in range(4):
-                qg[j // 4, j % 4, r * 2 + t // 2, pl.ds(t % 2 * TC, TC), :] = product[r * TC : (r + 1) * TC]
+                qg[j // 4, j % 4, r * 2 + t * TC // SPAN, pl.ds(t * TC % SPAN, TC), :] = product[r * TC : (r + 1) * TC]
             return carry
 
         lax.fori_loop(0, 8, tile, 0)
@@ -611,70 +631,93 @@
         chunks[t][1].relay(add_rows)
 
     def result(t):
-        chunks[t][1].end(
-            add_rows, lambda half: grad_encoded.at[pl.ds(half * 4, 4), pl.ds(t * TC, TC)]
-        )
-
+        unit = chunks[t][1]
+        for copy in unit.near:
+            copy.wait_recv()
+        for half in range(2):
+            for j in range(4):
+                cols = pl.ds(half * 2048 + j * 512, 512)
+                terms = (unit.part(ring_x.me, half)[j], x_got[half, t, j], x_got[2 + half, t, j])
+                grad_encoded[pl.ds(t * TC, TC), cols] = add_up(terms)
+
+    rows_complete()
+    unit_stats(0)
+    exchange_start(0)
+    spread(6)
+    unit_stats(1)
+    exchange_relay(0)
+    exchange_start(1)
+    spread(7)
+    early = list(copies.started.values())
+    exchange_end(0)
+    first_sends_done(0)
     attend_spans(0)
     zb(0, 0)
+    exchange_relay(1)
+    unit_stats(2)
+    exchange_start(2)
+    exchange_end(1)
+    first_sends_done(1)
     attend_spans(2)
     zr(0, 0)
     zb(1, 0)
+    exchange_relay(2)
+    unit_stats(3)
+    exchange_start(3)
+    exchange_end(2)
+    first_sends_done(2)
+    zd(0, 0)
+    attend_spans(4)
+    zr(1, 0)
     zb(0, 1)
-    attend_spans(4)
-    zd(0, 0)
-    zr(1, 0)
+    exchange_relay(3)
+    exchange_end(3)
+    first_sends_done(3)
+    zd(1, 0)
+    attend_spans(6)
     zr(0, 1)
     zb(1, 1)
-    attend_spans(6)
-    zd(1, 0)
+    for copy in early:
+        copies.settle(copy)
+    sister_rows(0)
+    zs(0, 0)
     zd(0, 1)
+    sister_rows(1)
+    zr(1, 1)
     zb(0, 2)
-    sister_rows(0)
-    zr(1, 1)
+    sister_rows(2)
+    zs(1, 0)
+    sister_rows(3)
+    zd(1, 1)
+    zr(0, 2)
     zb(1, 2)
-    zs(0, 0)
-    sister_rows(1)
-    zd(1, 1)
-    zs(1, 0)
-    sister_rows(2)
-    zr(0, 2)
-    zb(0, 3)
+    own_rows(0)
+    own_rows(1)
     zs(0, 1)
-    sister_rows(3)
     zd(0, 2)
     zr(1, 2)
-    zb(1, 3)
-    own_rows(0)
-    own_rows(1)
-    zd(1, 2)
-    zs(1, 1)
     own_rows(2)
     own_rows(3)
+    zb(0, 3)
     again = load_wide(0) + load_wide(1)
+    y_start(0)
+    zs(1, 1)
+    zd(1, 2)
     zr(0, 3)
-    y_start(0)
+    zb(1, 3)
+    zs(0, 2)
+    zd(0, 3)
+    y_relay(0)
     y_start(1)
-    zd(0, 3)
-    zs(0, 2)
+    zs(1, 2)
     zr(1, 3)
-    y_relay(0)
-    y_start(2)
     zd(1, 3)
-    zs(1, 2)
     y_done(0)
+    zs(0, 3)
     y_relay(1)
-    y_start(3)
-    zs(0, 3)
+    x_relay(0)
+    zs(1, 3)
     y_done(1)
-    x_relay(0)
-    y_relay(2)
-    zs(1, 3)
-    y_done(2)
-    x_relay(1)
-    y_relay(3)
-    x_relay(2)
-    y_done(3)
     for load in again:
         load.wait()
     for u in range(4):
@@ -690,7 +733,7 @@
             weight = wide[pl.ds(32 + j // 2 * 16 + g * 4, 4), :, cols].reshape(512, 256)
             term = dot(everyone(0, g, 0, 512), weight, 1, 0)
             total = term if total is None else total + term
-        attended[:, pl.ds(pl.multiple_of(j * 256, 256), 256)] = total.astype(BF)
+        v_hid[:, pl.ds(pl.multiple_of(j * 256, 256), 256)] = total.astype(BF)
         return carry
 
     def hidden_rows(first):
@@ -700,23 +743,34 @@
                 weight = wide[pl.ds(g * 8 + j * 2, 2)].reshape(256, 512)
                 term = dot(everyone(1, g, first, 256), weight, 1, 1)
                 total = term if total is None else total + term
-            grad_hidden[pl.ds(first, 256), pl.ds(pl.multiple_of(j * 256, 256), 256)] = total.astype(BF)
+            v_gout[pl.ds(first, 256), pl.ds(pl.multiple_of(j * 256, 256), 256)] = total.astype(BF)
             return carry
 
         lax.fori_loop(0, 4, tile, 0)
 
+    def shift_down(out, ref, t):
+        first = max(t - 1, 0) * 128
+        row = lax.broadcasted_iota(jnp.int32, (128, 256), 0) + (t * 128 - (SPAN - 1) - first)
+        col = lax.broadcasted_iota(jnp.int32, (128, 256), 1)
+        move = (row == col).astype(BF)
+        out[pl.ds(t * 128, 128), :] = dot(move, ref[pl.ds(first, 256), :], 1, 0).astype(BF)
+
     lax.fori_loop(0, 4, attended_tile, 0)
-    x_relay(3)
+    for t in range(4):
+        shift_down(attended, v_hid, t)
+    x_relay(1)
     result(0)
-    result(1)
-    result(2)
     for u in range(2):
         outs[1][u][1].end()
     hidden_rows(0)
+    for t in range(2):
+        shift_down(grad_hidden, v_gout, t)
     for u in range(2, 4):
         outs[1][u][1].end()
     hidden_rows(256)
-    result(3)
+    for t in range(2, 4):
+        shift_down(grad_hidden, v_gout, t)
+    result(1)
     copies.finish()
 
 
@@ -726,7 +780,7 @@
         out_shape=[
             jax.ShapeDtypeStruct((512, 1024), BF),
             jax.ShapeDtypeStruct((512, 1024), BF),
-            jax.ShapeDtypeStruct((8, NTOK, 512), BF),
+            jax.ShapeDtypeStruct((NTOK, 4096), BF),
             jax.ShapeDtypeStruct((4, 8, 128), jnp.int32),
         ],
         in_specs=[SM] + [ANY] * 8,
@@ -747,7 +801,7 @@
             pltpu.SMEM((4, 8, 128), jnp.int32),
             pltpu.SMEM((64,), jnp.int32),
             pltpu.SMEM((4, 32), jnp.int32),
-            pltpu.VMEM((3, 64, 128), F32),
+            pltpu.VMEM((2, 64, 128), F32),
             pltpu.VMEM((4, 3, 64, 128), F32),
             pltpu.VMEM((4, 2, 4, NTOK, 512), BF),
             pltpu.VMEM((2, CHUNKS, 4, TC, 512), BF),
@@ -755,8 +809,8 @@
             pltpu.VMEM((2, 4, TC, 512), BF),
             pltpu.VMEM((2, CHUNKS, 4, TC, 512), BF),
             pltpu.VMEM((4, CHUNKS, 4, TC, 512), BF),
-            pltpu.SemaphoreType.DMA((256,)),
-            pltpu.SemaphoreType.DMA((256,)),
+            pltpu.SemaphoreType.DMA((272,)),
+            pltpu.SemaphoreType.DMA((272,)),
             pltpu.SemaphoreType.DMA((40,)),
         ],
         compiler_params=pltpu.CompilerParams(
@@ -777,10 +831,6 @@
     )
 
 
-def shift_down(rows):
-    return jnp.pad(rows[: rows.shape[0] - SPAN + 1], ((SPAN - 1, 0), (0, 0)))
-
-
 def body(
     hidden, query_weight, key_weight, value_weight, output_weight,
     encoded, location, neighbours, pattern, grad_out,
@@ -790,8 +840,7 @@
         location, hidden, query_weight.reshape(8, 128, 2048), encoded.reshape(8, 64, 4096),
         key_weight, value_weight, grad_out, output_weight.reshape(16, 128, 1024), ids,
     )
-    grad_encoded = jnp.transpose(grad_encoded, (1, 0, 2)).reshape(1, NTOK, 4096)
-    return shift_down(attended), shift_down(grad_hidden), grad_encoded
+    return attended, grad_hidden, grad_encoded.reshape(1, NTOK, 4096)
 
 
 def solution(mesh):

time: 193 us -> 180 us (0.933)
  Pallas kernels: 183 us -> 172 us
    pallas_call x1, Pallas kernels: 183 us -> 172 us  [cross_attention(): pl.pallas_call(kernel, out_shape=[jax.ShapeDtypeStruct((512, 1024), BF),...]
    unnamed x7, local copies, waits for them, and re-layouts: 2.83 us -> 7.09 us
    pad x2 -> x0, local copies, waits for them, and re-layouts: 2.43 us -> none  [shift_down(): return jnp.pad(rows[:rows.shape[0] - SPAN + 1], ((SPAN - 1, 0), (0, 0)))]
where the time goes in v4:
time: 180 us
  Pallas kernels  172 us (96%)
  local copies, waits for them, and re-layouts  7.69 us (4%)
    pallas_call x1, Pallas kernels, cross_attention(): pl.pallas_call(kernel, out_shape=[jax.ShapeDtypeStruct((512, 1024), BF),...  172 us
    unnamed x7, local copies, waits for them, and re-layouts  7.09 us

profile of v4, /device:TPU:2, one launch (start us, length us, event | category | flops | bytes accessed | tf_op | source)
XLA Modules:
  0.0 179.9 jit_solution(8363262246465633537)
XLA Ops:
  0.6 0.8 copy.14
  1.4 0.8 copy.13
  2.1 0.6 pad.4.ids
  2.7 171.5 %cross_attention.1 = (bf16[512,1024]{1,0:T(8,128)(2,1)}, bf16[512,1024]{1,0:T(8,128)(2,1)}, bf16[128,4096]{1,0:T(8,128)(2,1)}, s32[4,8,128]{2,1,0:T(8,128)}) custom-call(s32[128]{0:T(128)} %loc_ref.1, bf16[512,1024]{1,0:T(8,128)(2,1)} %hid.1, bf16[8,128,2048]{2,1,0:T(8,128)(2,1)} %bitcast.4, bf16[8,64,4096]{2,1,0:T(8,128)(2,1)} %bitcast.5, ...), custom_call_target="tpu_custom_call" | custom-call | tf_op jit(solution)/shard_map/cross_attention/pallas_call | solution.py:778
  174.3 0.0 copy-start
  174.3 2.4 %copy.18 = bf16[512,1024]{1,0:T(8,128)(2,1)} copy(bf16[512,1024]{1,0:T(8,128)(2,1)} %get-tuple-element.12) | data formatting | bytes 2097152
  176.6 2.3 %copy.19 = bf16[512,1024]{1,0:T(8,128)(2,1)} copy(bf16[512,1024]{1,0:T(8,128)(2,1)} %get-tuple-element.13) | data formatting | bytes 2097152
  178.9 0.0 copy-done
  178.9 1.0 copy.20
  (1 shorter events, 0.0 us)
Async XLA Ops:
  174.3 4.6 %copy-start = (bf16[128,4096]{1,0:T(8,128)(2,1)S(1)}, bf16[128,4096]{1,0:T(8,128)(2,1)}, u32[]{:S(2)}) copy-start(bf16[128,4096]{1,0:T(8,128)(2,1)} %get-tuple-element.8) | copy-start | bytes 3145732
